TPU v7x, 128 devices: a whole 4x4x4 slice. The times are simulated.
128 devices in a mesh: dp: 8 (over y, core), tp: 16 (over z, x).
Axes of the slice: x: 4, y: 4, z: 4, core: 2. Of those that a mesh axis runs over, the one named last changes fastest.
Arguments:
- queries: bfloat16 [2, 1024, 128, 576], P(None, ('dp', 'tp')), may hold values from -11 to 11
- latent_cache: bfloat16 [1024, 512, 576], P(('dp', 'tp')), may hold values from -8 to 8
- lengths: int32 [1024], P(('dp', 'tp')), may hold values from 2 to 512, as said below
- inputs: bfloat16 [2, 1024, 4096], P(None, ('dp', 'tp')), may hold values from -9 to 9
- down_latent: bfloat16 [4096, 576], P('tp'), may hold values from -0.09375 to 0.09375
- value_up: bfloat16 [128, 512, 128], P('tp'), may hold values from -0.25 to 0.25
- output_weight: bfloat16 [16384, 4096], P('tp', 'dp'), may hold values from -0.125 to 0.125
- up_weight: bfloat16 [4096, 10240], P(None, 'tp'), may hold values from -0.09375 to 0.09375
- down_weight: bfloat16 [10240, 4096], P('tp'), may hold values from -0.0625 to 0.0625
Outputs:
- layer_out: bfloat16 [2, 1024, 4096], P(None, ('dp', 'tp'))
Inputs may be any that keep to these rules, and one draw needn't show every extreme that they name: Row r attends to cache positions below lengths[r]; some row uses all 512 positions.
All inputs are finite; a program needn't handle non-finite values.
Results may differ from a plain program's by a relative error of at most 0.023.
Values may be sent and summed in bfloat16 or wider, within the bound.
A program may use at most 128 MiB of HBM per device.

v0:
```python
import jax
import jax.numpy as jnp
from jax import lax
from jax.sharding import PartitionSpec as P

LAT = 512


EPSILON = 1e-06
SCORE_SCALE = 192.0 ** (-0.5)
ROPE_BASE = 10000.0


def mean_norm(values):
    return values * lax.rsqrt(jnp.mean(values * values, axis=-1, keepdims=True) + EPSILON)


def rotate_pairs(rope_part, positions):
    half_width = rope_part.shape[-1] // 2
    frequency = ROPE_BASE ** (-jnp.arange(half_width, dtype=jnp.float32) / half_width)
    angles = positions.astype(jnp.float32)[:, None] * frequency[None, :]
    first = rope_part[:, :half_width]
    second = rope_part[:, half_width:]
    cosine = jnp.cos(angles)
    sine = jnp.sin(angles)
    return jnp.concatenate(
        [first * cosine - second * sine, second * cosine + first * sine], axis=-1
    )


def finish_key(compressed, positions):
    latent_part = mean_norm(compressed[:, :LAT])
    rotated = rotate_pairs(compressed[:, LAT:], positions)
    return jnp.concatenate([latent_part, rotated], axis=-1).astype(jnp.bfloat16)


def attend(queries_now, latent_cache, lengths, new_keys):
    scores = (
        jnp.einsum("rhc,rlc->rhl", queries_now, latent_cache, preferred_element_type=jnp.float32)
        * SCORE_SCALE
    )
    valid = (jnp.arange(latent_cache.shape[1], dtype=jnp.int32)[None, :] < lengths[:, None])[
        :, None, :
    ]
    scores = jnp.where(valid, scores, jnp.float32(-1e30))
    fresh_scores = (
        jnp.einsum("rhc,rkc->rhk", queries_now, new_keys, preferred_element_type=jnp.float32)
        * SCORE_SCALE
    )
    maximum = jnp.maximum(jnp.max(scores, axis=-1), jnp.max(fresh_scores, axis=-1))[..., None]
    weights = jnp.where(valid, jnp.exp(scores - maximum), jnp.float32(0.0))
    fresh_weights = jnp.exp(fresh_scores - maximum)
    denominator = jnp.sum(weights, axis=-1, keepdims=True) + jnp.sum(
        fresh_weights, axis=-1, keepdims=True
    )
    probability = (weights / denominator).astype(jnp.bfloat16)
    fresh_probability = (fresh_weights / denominator).astype(jnp.bfloat16)
    combined = jnp.einsum(
        "rhl,rlc->rhc", probability, latent_cache, preferred_element_type=jnp.float32
    )
    combined = combined + jnp.einsum(
        "rhk,rkc->rhc", fresh_probability, new_keys, preferred_element_type=jnp.float32
    )
    return combined[..., :LAT].astype(jnp.bfloat16)


def body(
    queries,
    latent_cache,
    lengths,
    inputs,
    down_latent,
    value_up,
    output_weight,
    up_weight,
    down_weight,
):
    compressed = []
    for step in range(2):
        normed = mean_norm(inputs[step].astype(jnp.float32)).astype(jnp.bfloat16)
        pieces = lax.all_to_all(normed, "tp", split_axis=1, concat_axis=0, tiled=True)
        partial_terms = jnp.dot(pieces, down_latent, preferred_element_type=jnp.float32)
        compressed.append(
            lax.psum_scatter(
                partial_terms.astype(jnp.bfloat16), "tp", scatter_dimension=0, tiled=True
            ).astype(jnp.float32)
        )
    new_keys = []
    results = []
    for step in range(2):
        new_keys.append(finish_key(compressed[step], lengths + step))
        attended = attend(queries[step], latent_cache, lengths, jnp.stack(new_keys, axis=1))
        grouped = lax.all_to_all(attended, "tp", split_axis=1, concat_axis=0, tiled=True)
        values = jnp.einsum(
            "rhc,hcd->rhd", grouped, value_up, preferred_element_type=jnp.float32
        ).astype(jnp.bfloat16)
        values = values.reshape(values.shape[0], values.shape[1] * values.shape[2])
        attention_terms = jnp.dot(
            values,
            lax.all_gather(output_weight, "dp", axis=1, tiled=True),
            preferred_element_type=jnp.float32,
        )
        attention_mine = lax.psum_scatter(
            attention_terms.astype(jnp.bfloat16), "tp", scatter_dimension=0, tiled=True
        ).astype(jnp.float32)
        hidden_state = inputs[step].astype(jnp.float32) + attention_mine
        ffn_input = mean_norm(hidden_state).astype(jnp.bfloat16)
        activation = jax.nn.silu(
            jnp.dot(
                lax.all_gather(ffn_input, "tp", axis=0, tiled=True),
                up_weight,
                preferred_element_type=jnp.float32,
            )
        ).astype(jnp.bfloat16)
        ffn_terms = jnp.dot(activation, down_weight, preferred_element_type=jnp.float32)
        ffn_mine = lax.psum_scatter(
            ffn_terms.astype(jnp.bfloat16), "tp", scatter_dimension=0, tiled=True
        ).astype(jnp.float32)
        results.append((hidden_state + ffn_mine).astype(jnp.bfloat16))
    return jnp.stack(results, axis=0)


def solution(mesh):
    return jax.shard_map(
        body,
        mesh=mesh,
        in_specs=(
            P(None, ("dp", "tp"), None, None),
            P(("dp", "tp"), None, None),
            P(("dp", "tp")),
            P(None, ("dp", "tp"), None),
            P("tp", None),
            P("tp", None, None),
            P("tp", "dp"),
            P(None, "tp"),
            P("tp", None),
        ),
        out_specs=P(None, ("dp", "tp"), None),
        check_vma=False,
    )
```

profile of v0, /device:TPU:0, one launch (start us, length us, event | category | flops | bytes accessed | tf_op | source)
XLA Modules:
  0.0 638.7 jit_solution(6622558218197418847)
XLA Ops:
  7.4 1.0 slice_convert_fusion.1
  8.4 1.0 fusion.45
  9.4 0.1 multiply_convert_fusion.7
  9.4 15.4 %all_to_all.68 = bf16[8,16,256]{2,0,1:T(8,128)(2,1)S(1)} all-to-all(bf16[8,16,256]{2,0,1:T(8,128)(2,1)S(1)} %multiply_convert_fusion.7), channel_id=1, replica_groups=mesh['dp'=8,'tp'=16] {'tp'}, dimensions={1} | all-to-all | bytes 131072 | tf_op jit(solution)/shard_map/all_to_all | solution.py:81
  24.9 1.9 convolution_convert_fusion.7
  26.8 0.0 all-reduce.13.cloned.1.call-update
  26.8 0.0 all-gather.4.cloned.1.call-start
  26.8 0.5 all-gather.4.cloned.1.call-update
  27.4 0.0 all-reduce.15.cloned.1.call-start
  27.4 0.6 dynamic-slice
  28.7 0.1 iota_compare_fusion
  28.8 3.9 fusion.2
  32.7 75.7 %all-reduce.13.cloned.1.call-done = bf16[128,576]{1,0:T(8,128)(2,1)} async-done(((bf16[128,576]{1,0:T(8,128)(2,1)}), bf16[128,576]{1,0:T(8,128)(2,1)}) %all-reduce.13.cloned.1.call-update) | async-done | bytes 147472
  108.3 0.7 dynamic-slice_convert_fusion.1
  109.0 0.1 multiply_reduce_fusion.3
  109.2 0.1 fusion.67
  109.3 0.1 multiply_convert_fusion.9
  109.3 0.1 fusion.72
  109.4 1.7 fusion.10
  111.1 5.8 fusion.4
  116.9 2.0 fusion.20
  118.9 0.3 fusion.1
  119.2 0.6 copy.76
  119.8 19.9 %all_to_all.69 = bf16[8,128,512]{2,0,1:T(8,128)(2,1)S(1)} all-to-all(bf16[8,128,512]{2,0,1:T(8,128)(2,1)S(1)} %copy.76), channel_id=1, replica_groups=mesh['dp'=8,'tp'=16] {'tp'}, dimensions={1} | all-to-all | bytes 2097152 | tf_op jit(solution)/shard_map/all_to_all | solution.py:93
  139.7 0.5 convolution_convert_fusion.5
  140.2 0.0 all-gather.4.cloned.1.call-done
  140.2 5.7 convolution_convert_fusion.3
  145.9 0.0 all-reduce.15.cloned.1.call-update
  145.9 0.0 all-reduce.17.cloned.1.call-start
  146.0 84.6 %all-reduce.15.cloned.1.call-done = bf16[128,4096]{1,0:T(8,128)(2,1)} async-done(((bf16[128,4096]{1,0:T(8,128)(2,1)}), bf16[128,4096]{1,0:T(8,128)(2,1)}) %all-reduce.15.cloned.1.call-update) | async-done | bytes 1048592
  230.6 1.0 multiply_reduce_fusion.1
  231.7 0.1 multiply_convert_fusion.5
  231.7 12.3 %all_to_all.70 = bf16[8,16,256]{2,0,1:T(8,128)(2,1)S(1)} all-to-all(bf16[8,16,256]{2,0,1:T(8,128)(2,1)S(1)} %multiply_convert_fusion.5), channel_id=1, replica_groups=mesh['dp'=8,'tp'=16] {'tp'}, dimensions={1} | all-to-all | bytes 131072 | tf_op jit(solution)/shard_map/all_to_all | solution.py:81
  244.0 1.9 convolution_convert_fusion.6
  245.9 0.0 all-reduce.19.cloned.1.call-start
  246.0 0.1 fusion.109
  246.1 81.1 %all-reduce.17.cloned.1.call-done = bf16[128,576]{1,0:T(8,128)(2,1)} async-done(((bf16[128,576]{1,0:T(8,128)(2,1)}), bf16[128,576]{1,0:T(8,128)(2,1)}) %all-reduce.17.cloned.1.call-update) | async-done | bytes 147472
  327.2 0.7 dynamic-slice_convert_fusion
  327.9 0.1 multiply_reduce_fusion.2
  328.0 0.1 fusion.51
  328.1 0.1 fusion.76
  328.3 1.6 fusion.86
  330.0 0.7 fusion.5
  330.7 4.0 fusion.21
  334.7 0.6 fusion.61
  335.3 0.4 fusion
  335.6 0.6 copy.85
  336.2 19.9 %all_to_all.71 = bf16[8,128,512]{2,0,1:T(8,128)(2,1)S(1)} all-to-all(bf16[8,128,512]{2,0,1:T(8,128)(2,1)S(1)} %copy.85), channel_id=1, replica_groups=mesh['dp'=8,'tp'=16] {'tp'}, dimensions={1} | all-to-all | bytes 2097152 | tf_op jit(solution)/shard_map/all_to_all | solution.py:93
  356.1 0.5 convolution_convert_fusion.4
  356.6 2.3 convolution_convert_fusion.1
  359.0 0.0 all-gather.8.cloned.1.call-start
  359.1 84.6 %all-reduce.19.cloned.1.call-done = bf16[128,4096]{1,0:T(8,128)(2,1)} async-done(((bf16[128,4096]{1,0:T(8,128)(2,1)}), bf16[128,4096]{1,0:T(8,128)(2,1)}) %all-reduce.19.cloned.1.call-update) | async-done | bytes 1048592
  443.6 1.0 multiply_reduce_fusion
  444.6 1.6 multiply_convert_fusion.6
  446.3 0.0 all-gather.6.cloned.1.call-start
  446.3 0.5 all-gather.6.cloned.1.call-update
  446.8 0.0 all-reduce.21.cloned.1.call-start
  446.9 41.5 %all-gather.8.cloned.1.call-done = bf16[128,4096]{1,0:T(8,128)(2,1)} async-done(((bf16[8,4096]{1,0:T(8,128)(2,1)}), bf16[128,4096]{1,0:T(8,128)(2,1)}) %all-gather.8.cloned.1.call-update) | async-done | bytes 1048592 | tf_op jit(solution)/shard_map/all_gather | solution.py:110
  488.4 7.2 %convolution_convert_fusion = bf16[128,4096]{1,0:T(8,128)(2,1)} fusion(bf16[640,4096]{1,0:T(8,128)(2,1)} %param.17, bf16[128,4096]{1,0:T(8,128)(2,1)} %all-gather.8.cloned.1.call-done, bf16[4096,640]{1,0:T(8,128)(2,1)} %param.16), kind=kOutput, calls=%fused_computation | convolution fusion | flops 1343111168 | bytes 12582912 | tf_op jit(solution)/shard_map/dot_general | solution.py:115
  495.6 36.9 %all-gather.6.cloned.1.call-done = bf16[128,4096]{1,0:T(8,128)(2,1)} async-done(((bf16[8,4096]{1,0:T(8,128)(2,1)}), bf16[128,4096]{1,0:T(8,128)(2,1)}) %all-gather.6.cloned.1.call-update) | async-done | bytes 1048592 | tf_op jit(solution)/shard_map/all_gather | solution.py:110
  532.6 7.2 %convolution_convert_fusion.2 = bf16[128,4096]{1,0:T(8,128)(2,1)} fusion(bf16[640,4096]{1,0:T(8,128)(2,1)} %param.17, bf16[128,4096]{1,0:T(8,128)(2,1)} %all-gather.6.cloned.1.call-done, bf16[4096,640]{1,0:T(8,128)(2,1)} %param.16), kind=kOutput, calls=%fused_computation.2 | convolution fusion | flops 1343111168 | bytes 12582912 | tf_op jit(solution)/shard_map/dot_general | solution.py:115
  539.8 89.8 %all-reduce.21.cloned.1.call-done = (bf16[128,4096]{1,0:T(8,128)(2,1)}, bf16[128,4096]{1,0:T(8,128)(2,1)}) async-done(((bf16[128,4096]{1,0:T(8,128)(2,1)}, bf16[128,4096]{1,0:T(8,128)(2,1)}), (bf16[128,4096]{1,0:T(8,128)(2,1)}, bf16[128,4096]{1,0:T(8,128)(2,1)})) %all-reduce.21.cloned.1.call-update) | async-done | bytes 2097168
  629.6 1.0 fusion.46
  630.6 0.6 copy-done.4
  (47 shorter events, 0.3 us)
Async XLA Ops:
  7.4 132.3 %copy-start = (bf16[8,512,128]{2,1,0:T(8,128)(2,1)S(1)}, bf16[8,512,128]{2,1,0:T(8,128)(2,1)}, u32[]{:S(2)}) copy-start(bf16[8,512,128]{2,1,0:T(8,128)(2,1)} %param.14) | copy-start | bytes 3145732
  7.4 20.0 %copy-start.5 = (u32[128]{0:T(128)S(1)}, u32[128]{0:T(128)}, u32[]{:S(2)}) copy-start(u32[128]{0:T(128)} %constant.40) | copy-start | bytes 1540
  7.4 21.3 %copy-start.3 = (s32[8]{0:T(128)S(1)}, s32[8]{0:T(128)}, u32[]{:S(2)}) copy-start(s32[8]{0:T(128)} %param.11) | copy-start | bytes 100
  7.4 100.9 %all-reduce.13.cloned.1.call-start = ((), (), s32[]{:S(2)}) async-start(), calls=%async_computation.7 | async-start | bytes 327680
  26.8 113.4 %all-gather.4.cloned.1.call-start = ((), (), s32[]{:S(2)}) async-start(), calls=%async_computation.4 | async-start | bytes 9437184 | tf_op jit(solution)/shard_map/all_gather | solution.py:100
  27.4 203.3 %all-reduce.15.cloned.1.call-start = ((), (), s32[]{:S(2)}) async-start(), calls=%async_computation.8 | async-start | bytes 2097152
  109.4 7.5 %slice-start.2 = ((s8[4718592]{0:T(1024)(128)(4,1)}), s8[4194304]{0:T(1024)(128)(4,1)S(1)}, s32[]{:S(2)}) async-start(s8[4718592]{0:T(1024)(128)(4,1)} %bitcast.113), calls=%async_computation.14 | async-start | bytes 8388608
  111.1 5.8 slice-start.3
  140.2 90.4 %copy-start.1 = (bf16[2,8,4096]{2,1,0:T(8,128)(2,1)S(1)}, bf16[2,8,4096]{2,1,0:T(8,128)(2,1)}, u32[]{:S(2)}) copy-start(bf16[2,8,4096]{2,1,0:T(8,128)(2,1)} %param.12) | copy-start | bytes 393220
  145.9 184.0 %copy-start.2 = (f32[8,128,512]{2,1,0:T(8,128)S(1)}, f32[8,128,512]{2,1,0:T(8,128)}, u32[]{:S(2)}) copy-start(f32[8,128,512]{2,1,0:T(8,128)} %get-tuple-element.29) | copy-start | bytes 6291460
  145.9 181.3 %all-reduce.17.cloned.1.call-start = ((), (), s32[]{:S(2)}) async-start(), calls=%async_computation.9 | async-start | bytes 327680
  245.9 197.7 %all-reduce.19.cloned.1.call-start = ((), (), s32[]{:S(2)}) async-start(), calls=%async_computation.10 | async-start | bytes 2097152
  329.9 26.7 %slice-start = ((s8[8388608]{0:T(1024)(128)(4,1)}), s8[4194304]{0:T(1024)(128)(4,1)S(1)}, s32[]{:S(2)}) async-start(s8[8388608]{0:T(1024)(128)(4,1)} %bitcast.111), calls=%async_computation.12 | async-start | bytes 8388608
  330.7 26.0 %slice-start.1 = ((s8[8388608]{0:T(1024)(128)(4,1)}), s8[4194304]{0:T(1024)(128)(4,1)S(1)}, s32[]{:S(2)}) async-start(s8[8388608]{0:T(1024)(128)(4,1)} %bitcast.111), calls=%async_computation.13 | async-start | bytes 8388608
  359.0 129.4 %all-gather.8.cloned.1.call-start = ((), (), s32[]{:S(2)}) async-start(), calls=%async_computation.6 | async-start | bytes 1114112 | tf_op jit(solution)/shard_map/all_gather | solution.py:110
  446.3 86.3 %all-gather.6.cloned.1.call-start = ((), (), s32[]{:S(2)}) async-start(), calls=%async_computation.5 | async-start | bytes 1114112 | tf_op jit(solution)/shard_map/all_gather | solution.py:110
  446.8 182.7 %all-reduce.21.cloned.1.call-start = ((), (), s32[]{:S(2)}) async-start(), calls=%async_computation.11 | async-start | bytes 4194304
  630.6 0.7 copy-start.4
Sparse Core Ops, SparseCore 0:
  26.9 81.3 all-reduce.12
  146.1 84.5 all-reduce.14
  246.0 81.1 all-reduce.16
  359.1 84.4 all-reduce.18
  446.4 41.9 all-gather.7
  490.4 42.0 all-gather.5
  539.9 89.6 all-reduce.20
Sparse Core Ops, SparseCore 1:
  28.9 47.4 all-gather.3
where the time goes:
time: 639 us
  waiting for transfers between devices  495 us (77%)
  blocking collectives  67.5 us (11%)
  matrix products  46.7 us (7%)
  between operations  15.9 us (2%)
  other arithmetic  10.4 us (2%)
    unnamed x13, waiting for transfers between devices  417 us
    all_gather x2, waiting for transfers between devices, body(): lax.all_gather(ffn_input, 'tp', axis=0, tiled=True)  78.4 us
    all_to_all x2, blocking collectives, body(): lax.all_to_all(attended, 'tp', split_axis=1, concat_axis=0, tiled=True)  39.8 us
    all_to_all x2, blocking collectives, body(): lax.all_to_all(normed, 'tp', split_axis=1, concat_axis=0, tiled=True)  27.7 us
    dot_general x2, matrix products, body(): jnp.dot(activation, down_weight, preferred_element_type=jnp.float32)  14.4 us
  transfers between devices with their start and end apart: 8, of which 7 were waited for; matrix products, arithmetic and copies ran while one was open for 4% of the time, Pallas kernels for 0%

commit v1 on v0

v1 whole, which is shorter than its diff:
```python
import jax
import jax.numpy as jnp
from jax import lax
from jax.experimental import pallas as pl
from jax.experimental.pallas import tpu as pltpu
from jax.sharding import PartitionSpec as P

LAT = 512
WIDTH = 576
CTX = 512
D = 4096
FF = 640
EPSILON = 1e-06
SCORE_SCALE = 192.0 ** (-0.5)
ROPE_BASE = 10000.0
NEG = -1e30
BF = jnp.bfloat16
F32 = jnp.float32
MESH = pl.DeviceIdType.MESH

PLANE = (
    (0, 1), (0, 3), (1, 0), (3, 0), (2, 1), (1, 2), (2, 3), (3, 2),
    (2, 2), (1, 1), (3, 3), (1, 3), (3, 1), (0, 2), (2, 0),
)
LINE = (1, 3, 2)


def copy_to(src, dst, send_sem, recv_sem, device):
    return pltpu.make_async_remote_copy(
        src_ref=src, dst_ref=dst, send_sem=send_sem, recv_sem=recv_sem,
        device_id=device, device_id_type=MESH,
    )


def kernel(
    lens, x_in, cos_in, sin_in, q_hbm, c_hbm, dl_hbm, vu_hbm, ow_hbm, up_hbm, dn_hbm,
    out,
    q_v, c_v, dl_v, vu_v, w_v, up_v, dn_v,
    xs, xr, ps, pr, keys_b, keys_f, o_v, m_v, l_v,
    send_a, recv_a, val_f, val_b,
    c_send1, c_recv1, c_send2, c_recv2, hid, gath, acc, act,
    e_send1, e_recv1, e_send2, e_recv2,
    sem_q, sem_c, sem_w, sem_vu,
    ss_x, rs_x, ss_p, rs_p, ss_a, rs_a, ss_w, rs_w,
    ss_c1, rs_c1, ss_c2, rs_c2, ss_g, rs_g, ss_e1, rs_e1, ss_e2, rs_e2,
):
    dp = lax.axis_index("dp")
    tp = lax.axis_index("tp")
    y, core = dp // 2, dp % 2
    z, x = tp // 4, tp % 4
    plane = [((z + dz) % 4) * 4 + (x + dx) % 4 for dz, dx in PLANE]
    on_x = [z * 4 + (x + k) % 4 for k in LINE]
    on_z = [((z + k) % 4) * 4 + x for k in LINE]
    y_up, y_dn, y_far = (y + 1) % 4, (y + 3) % 4, (y + 2) % 4
    sibling = y * 2 + 1 - core

    def q_copy(r):
        return pltpu.make_async_copy(q_hbm.at[:, r], q_v.at[:, r], sem_q.at[r])

    def c_copy(r):
        return pltpu.make_async_copy(c_hbm.at[r], c_v.at[r], sem_c.at[r])

    dl_copy = pltpu.make_async_copy(dl_hbm, dl_v, sem_w.at[0])
    ow_copy = pltpu.make_async_copy(ow_hbm, w_v.at[dp], sem_w.at[1])
    up_copy = pltpu.make_async_copy(up_hbm, up_v, sem_w.at[2])
    dn_copy = pltpu.make_async_copy(dn_hbm, dn_v, sem_w.at[3])
    vu_copies = [
        pltpu.make_async_copy(vu_hbm.at[h], vu_v.at[:, pl.ds(h * 128, 128)], sem_vu.at[h])
        for h in range(8)
    ]
    for r in range(8):
        q_copy(r).start()
        c_copy(r).start()
        if r == 1:
            dl_copy.start()

    barrier = pltpu.get_barrier_semaphore()
    partners = [(dp, t) for t in plane] + [
        (sibling, tp), (y_up * 2 + core, tp), (y_dn * 2 + core, tp)
    ]
    for device in partners:
        pl.semaphore_signal(barrier, inc=1, device_id=device, device_id_type=MESH)

    x0 = jnp.concatenate([x_in[0].astype(F32), x_in[1].astype(F32)], axis=0)
    scale = lax.rsqrt(jnp.mean(x0 * x0, axis=-1, keepdims=True) + EPSILON)
    xn = (x0 * scale).astype(BF)
    for t in range(16):
        xs[t] = xn[:, t * 256:(t + 1) * 256]
    xr[tp] = xs[tp]

    pl.semaphore_wait(barrier, len(partners))

    x_copies = [
        copy_to(xs.at[t], xr.at[tp], ss_x.at[k], rs_x.at[k], (dp, t))
        for k, t in enumerate(plane)
    ]
    for c in x_copies:
        c.start()

    lo, hi = pl.ds(0, 512), pl.ds(512, 512)
    up_dev, dn_dev, sib_dev = (y_up * 2 + core, tp), (y_dn * 2 + core, tp), (sibling, tp)
    w_up = [
        copy_to(ow_hbm.at[s], w_v.at[dp, s], ss_w.at[i], rs_w.at[i], up_dev)
        for i, s in enumerate((lo, hi))
    ]
    w_dn = [
        copy_to(ow_hbm.at[s], w_v.at[dp, s], ss_w.at[2 + i], rs_w.at[2 + i], dn_dev)
        for i, s in enumerate((hi, lo))
    ]
    w_sib = copy_to(ow_hbm, w_v.at[dp], ss_w.at[4], rs_w.at[4], sib_dev)
    from_dn, from_up, from_far = y_dn * 2 + core, y_up * 2 + core, y_far * 2 + core
    w_up2 = copy_to(w_v.at[from_dn, lo], w_v.at[from_dn, lo], ss_w.at[5], rs_w.at[5], up_dev)
    w_dn2 = copy_to(w_v.at[from_up, hi], w_v.at[from_up, hi], ss_w.at[6], rs_w.at[6], dn_dev)
    w_sib_dn = copy_to(w_v.at[from_dn], w_v.at[from_dn], ss_w.at[7], rs_w.at[7], sib_dev)
    w_sib_up = copy_to(w_v.at[from_up], w_v.at[from_up], ss_w.at[8], rs_w.at[8], sib_dev)
    w_sib_far = copy_to(w_v.at[from_far], w_v.at[from_far], ss_w.at[9], rs_w.at[9], sib_dev)
    for c in (w_up[0], w_dn[0], w_up[1], w_dn[1], w_sib):
        c.start()
    ow_copy.start()

    def attend_row(r, carry):
        q_copy(r).wait()
        c_copy(r).wait()
        q = jnp.concatenate([q_v[0, r], q_v[1, r]], axis=0)
        k = c_v[r]
        s = lax.dot_general(
            q, k, (((1,), (1,)), ((), ())), preferred_element_type=F32
        ) * SCORE_SCALE
        position = lax.broadcasted_iota(jnp.int32, (1, CTX), 1)
        s = jnp.where(position < lens[r], s, NEG)
        m = jnp.max(s, axis=-1, keepdims=True)
        p = jnp.exp(s - m)
        l_v[r] = jnp.sum(p, axis=-1, keepdims=True)
        m_v[r] = m
        o_v[r] = jnp.dot(p.astype(BF), k[:, :LAT], preferred_element_type=F32)
        return carry

    lax.fori_loop(0, 4, attend_row, 0)

    for c in vu_copies:
        c.start()
    up_copy.start()
    dn_copy.start()

    dl_copy.wait()
    for c in x_copies:
        c.wait_recv()
    partial = jnp.dot(xr[...].reshape(256, 256), dl_v[...], preferred_element_type=F32)
    ps[...] = partial.astype(BF).reshape(16, 16, WIDTH)
    p_copies = [
        copy_to(ps.at[t], pr.at[k], ss_p.at[k], rs_p.at[k], (dp, t))
        for k, t in enumerate(plane)
    ]
    for c in p_copies:
        c.start()

    lax.fori_loop(4, 8, attend_row, 0)

    for c in p_copies:
        c.wait_recv()
    comp = ps[tp].astype(F32)
    for k in range(15):
        comp = comp + pr[k].astype(F32)
    lat = comp[:, :LAT]
    lat = lat * lax.rsqrt(jnp.mean(lat * lat, axis=-1, keepdims=True) + EPSILON)
    rope = comp[:, LAT:]
    swapped = jnp.concatenate([rope[:, 32:], rope[:, :32]], axis=-1)
    rotated = rope * cos_in[...] + swapped * sin_in[...]
    keys_b[:, :LAT] = lat.astype(BF)
    keys_b[:, LAT:] = rotated.astype(BF)
    keys_f[...] = lat.astype(BF).astype(F32)

    def a_copies(i):
        rows = pl.ds(2 * i, 2)
        return [
            copy_to(send_a.at[rows, t], recv_a.at[rows, tp], ss_a.at[i, k], rs_a.at[i, k], (dp, t))
            for k, t in enumerate(plane)
        ]

    def finish_row(r):
        q = jnp.concatenate([q_v[0, r], q_v[1, r]], axis=0)
        fresh = lax.dot_general(
            q, keys_b[...], (((1,), (1,)), ((), ())), preferred_element_type=F32
        ) * SCORE_SCALE
        lane = lax.broadcasted_iota(jnp.int32, (256, 16), 1)
        row = lax.broadcasted_iota(jnp.int32, (256, 1), 0)
        s0 = jnp.sum(jnp.where(lane == r, fresh, 0.0), axis=-1, keepdims=True)
        s1 = jnp.sum(jnp.where(lane == r + 8, fresh, 0.0), axis=-1, keepdims=True)
        s1 = jnp.where(row >= 128, s1, NEG)
        m_old = m_v[r]
        m = jnp.maximum(jnp.maximum(m_old, s0), s1)
        keep = jnp.exp(m_old - m)
        p0 = jnp.exp(s0 - m)
        p1 = jnp.exp(s1 - m)
        inverse = 1.0 / (keep * l_v[r] + p0 + p1)
        k0 = keys_f[pl.ds(r, 1), :]
        k1 = keys_f[pl.ds(r + 8, 1), :]
        o = o_v[r] * (keep * inverse) + (p0 * inverse) * k0 + (p1 * inverse) * k1
        pieces = []
        for t in range(16):
            pieces += [o[t * 8:t * 8 + 8], o[128 + t * 8:128 + t * 8 + 8]]
        send_a[r] = jnp.concatenate(pieces, axis=0).astype(BF).reshape(16, 16, LAT)
        recv_a[r, tp] = send_a[r, tp]

    def finish_pair(i, carry):
        finish_row(2 * i)
        finish_row(2 * i + 1)
        for c in a_copies(i):
            c.start()
        return carry

    lax.fori_loop(0, 4, finish_pair, 0)

    w_up[0].wait_recv()
    w_up2.start()
    w_dn[0].wait_recv()
    w_dn2.start()
    w_up[1].wait_recv()
    w_sib_dn.start()
    w_dn[1].wait_recv()
    w_sib_up.start()

    for c in vu_copies:
        c.wait()

    def values_pair(i, carry):
        for c in a_copies(i):
            c.wait_recv()
        head = lax.broadcasted_iota(jnp.int32, (8, 128), 0)[None]
        for j in range(2):
            a = recv_a[2 * i + j].reshape(256, LAT)
            full = jnp.dot(a, vu_v[...], preferred_element_type=F32)
            full = full.reshape(32, 8, 1024)
            own = jnp.where(head == 0, full[:, :, :128], 0.0)
            for h in range(1, 8):
                own = jnp.where(head == h, full[:, :, h * 128:(h + 1) * 128], own)
            for b in range(32):
                at = pl.multiple_of(b * 64 + (2 * i + j) * 8, 8)
                val_f[pl.ds(at, 8), :] = own[b]
        return carry

    lax.fori_loop(0, 4, values_pair, 0)
    for h in range(8):
        val_b[:, h * 128:(h + 1) * 128] = val_f[pl.ds(h, 256, stride=8), :].astype(BF)

    w_up2.wait_recv()
    w_dn2.wait_recv()
    w_sib_far.start()
    ow_copy.wait()

    def stage1(i, send1, recv1, ss, rs):
        first = [
            copy_to(send1.at[i, 0, :, (x + k) % 4], recv1.at[i, 0, n],
                    ss.at[i, 0, n], rs.at[i, 0, n], (dp, on_x[n]))
            for n, k in enumerate(LINE)
        ]
        second = [
            copy_to(send1.at[i, 1, (z + k) % 4], recv1.at[i, 1, n],
                    ss.at[i, 1, n], rs.at[i, 1, n], (dp, on_z[n]))
            for n, k in enumerate(LINE)
        ]
        return first + second

    def stage2(i, send2, recv2, ss, rs):
        first = [
            copy_to(send2.at[i, 0, (z + k) % 4], recv2.at[i, 0, n],
                    ss.at[i, 0, n], rs.at[i, 0, n], (dp, on_z[n]))
            for n, k in enumerate(LINE)
        ]
        second = [
            copy_to(send2.at[i, 1, (x + k) % 4], recv2.at[i, 1, n],
                    ss.at[i, 1, n], rs.at[i, 1, n], (dp, on_x[n]))
            for n, k in enumerate(LINE)
        ]
        return first + second

    def group_sum(multiply, before, send1, recv1, send2, recv2, ss1, rs1, ss2, rs2):
        def middle(i):
            for c in stage1(i, send1, recv1, ss1, rs1):
                c.wait_recv()
            for way, own in ((0, send1[i, 0, :, x]), (1, send1[i, 1, z])):
                total = own.astype(F32)
                for n in range(3):
                    total = total + recv1[i, way, n].astype(F32)
                send2[i, way] = total.astype(BF)
            for c in stage2(i, send2, recv2, ss2, rs2):
                c.start()

        def step(i, carry):
            before(i)
            for way in range(2):
                send1[i, way] = multiply(i, way).astype(BF).reshape(4, 4, 16, 512)
            for c in stage1(i, send1, recv1, ss1, rs1):
                c.start()

            @pl.when(i > 0)
            def _():
                middle(i - 1)

            return carry

        lax.fori_loop(0, 4, step, 0)
        middle(3)

    def summed(i, way, send2, recv2):
        total = send2[i, way, z if way == 0 else x].astype(F32)
        for n in range(3):
            total = total + recv2[i, way, n].astype(F32)
        return total

    def block_of(i):
        return (y + i + i // 2 - 2 * (i // 3)) % 4

    def before_c(i):
        @pl.when(i == 0)
        def _():
            w_sib.wait_recv()

        @pl.when(i == 1)
        def _():
            w_sib_up.wait_recv()

        @pl.when(i == 2)
        def _():
            w_sib_dn.wait_recv()

        @pl.when(i == 3)
        def _():
            w_sib_far.wait_recv()

    group_sum(
        lambda i, way: jnp.dot(
            val_b[...], w_v[block_of(i) * 2 + way], preferred_element_type=F32
        ),
        before_c, c_send1, c_recv1, c_send2, c_recv2, ss_c1, rs_c1, ss_c2, rs_c2,
    )

    def take_c(i, carry):
        for c in stage2(i, c_send2, c_recv2, ss_c2, rs_c2):
            c.wait_recv()
        for way in range(2):
            hid[block_of(i) * 2 + way] = summed(i, way, c_send2, c_recv2)
        return carry

    lax.fori_loop(0, 4, take_c, 0)

    square = jnp.zeros((16, 1), F32)
    for j in range(8):
        cols = slice(j * 512, (j + 1) * 512)
        part = jnp.concatenate([x_in[0, :, cols].astype(F32), x_in[1, :, cols].astype(F32)], axis=0)
        part = part + hid[j]
        hid[j] = part
        square = square + jnp.sum(part * part, axis=-1, keepdims=True)
    scale = lax.rsqrt(square / D + EPSILON)
    for j in range(8):
        gath[j // 4, z, x, :, (j % 4) * 512:(j % 4 + 1) * 512] = (hid[j] * scale).astype(BF)

    def g_copy(way, at_z, at_x, device, n):
        block = gath.at[way, at_z, at_x]
        return copy_to(block, block, ss_g.at[way, n], rs_g.at[way, n], (dp, device))

    g_first = [
        [g_copy(0, z, x, on_x[n], n) for n in range(3)],
        [g_copy(1, z, x, on_z[n], n) for n in range(3)],
    ]
    g_own = [
        [g_copy(0, z, x, on_z[n], 3 + n) for n in range(3)],
        [g_copy(1, z, x, on_x[n], 3 + n) for n in range(3)],
    ]
    for n in range(3):
        for way in range(2):
            g_first[way][n].start()
    for n in range(3):
        for way in range(2):
            g_own[way][n].start()
    g_pass = [[], []]
    for m, k in enumerate(LINE):
        g_first[0][m].wait_recv()
        for n in range(3):
            c = g_copy(0, z, (x + 4 - k) % 4, on_z[n], 6 + 3 * m + n)
            c.start()
            g_pass[0].append(c)
        g_first[1][m].wait_recv()
        for n in range(3):
            c = g_copy(1, (z + 4 - k) % 4, x, on_x[n], 6 + 3 * m + n)
            c.start()
            g_pass[1].append(c)

    up_copy.wait()
    acc[...] = jnp.zeros_like(acc)
    for way in range(2):
        for c in g_own[way] + g_pass[way]:
            c.wait_recv()
        for j in range(4):
            a = gath[way, :, :, :, j * 512:(j + 1) * 512].reshape(256, 512)
            at = way * 2048 + j * 512
            acc[...] += jnp.dot(a, up_v[at:at + 512, :], preferred_element_type=F32)
    v = acc[...]
    act[...] = (v / (1.0 + jnp.exp(-v))).astype(BF)

    dn_copy.wait()
    group_sum(
        lambda i, way: jnp.dot(
            act[...], dn_v[:, pl.ds(pl.multiple_of(i * 1024 + way * 512, 512), 512)],
            preferred_element_type=F32,
        ),
        lambda i: None, e_send1, e_recv1, e_send2, e_recv2, ss_e1, rs_e1, ss_e2, rs_e2,
    )
    for i in range(4):
        for c in stage2(i, e_send2, e_recv2, ss_e2, rs_e2):
            c.wait_recv()
        for way in range(2):
            total = hid[2 * i + way] + summed(i, way, e_send2, e_recv2)
            cols = slice(i * 1024 + way * 512, i * 1024 + (way + 1) * 512)
            out[0, :, cols] = total[:8].astype(BF)
            out[1, :, cols] = total[8:].astype(BF)

    for c in x_copies + p_copies:
        c.wait_send()

    def drain(i, carry):
        for c in a_copies(i):
            c.wait_send()
        for c in stage1(i, c_send1, c_recv1, ss_c1, rs_c1) + stage2(i, c_send2, c_recv2, ss_c2, rs_c2):
            c.wait_send()
        for c in stage1(i, e_send1, e_recv1, ss_e1, rs_e1) + stage2(i, e_send2, e_recv2, ss_e2, rs_e2):
            c.wait_send()
        return carry

    lax.fori_loop(0, 4, drain, 0)
    for c in w_up + w_dn + [w_sib, w_up2, w_dn2, w_sib_dn, w_sib_up, w_sib_far]:
        c.wait_send()
    for way in range(2):
        for c in g_first[way] + g_own[way] + g_pass[way]:
            c.wait_send()


def layer(lengths, inputs, cosine, sine, queries, cache, down_latent, value_up, output_weight, up_weight, down_weight):
    vmem, hbm = pl.BlockSpec(memory_space=pltpu.VMEM), pl.BlockSpec(memory_space=pl.ANY)
    dma = pltpu.SemaphoreType.DMA
    scratch = [
        pltpu.VMEM((2, 8, 128, WIDTH), BF),
        pltpu.VMEM((8, CTX, WIDTH), BF),
        pltpu.VMEM((256, WIDTH), BF),
        pltpu.VMEM((LAT, 1024), BF),
        pltpu.VMEM((8, 1024, 512), BF),
        pltpu.VMEM((D, FF), BF),
        pltpu.VMEM((FF, D), BF),
        pltpu.VMEM((16, 16, 256), BF),
        pltpu.VMEM((16, 16, 256), BF),
        pltpu.VMEM((16, 16, WIDTH), BF),
        pltpu.VMEM((15, 16, WIDTH), BF),
        pltpu.VMEM((16, WIDTH), BF),
        pltpu.VMEM((16, LAT), F32),
        pltpu.VMEM((8, 256, LAT), F32),
        pltpu.VMEM((8, 256, 1), F32),
        pltpu.VMEM((8, 256, 1), F32),
        pltpu.VMEM((8, 16, 16, LAT), BF),
        pltpu.VMEM((8, 16, 16, LAT), BF),
        pltpu.VMEM((2048, 128), F32),
        pltpu.VMEM((256, 1024), BF),
    ]
    sums = [
        pltpu.VMEM((4, 2, 4, 4, 16, 512), BF),
        pltpu.VMEM((4, 2, 3, 4, 16, 512), BF),
        pltpu.VMEM((4, 2, 4, 16, 512), BF),
        pltpu.VMEM((4, 2, 3, 16, 512), BF),
    ]
    scratch += sums + [
        pltpu.VMEM((8, 16, 512), F32),
        pltpu.VMEM((2, 4, 4, 16, 2048), BF),
        pltpu.VMEM((256, FF), F32),
        pltpu.VMEM((256, FF), BF),
    ] + sums
    scratch += [dma((8,)), dma((8,)), dma((4,)), dma((8,))]
    scratch += [dma((15,))] * 4 + [dma((4, 15))] * 2 + [dma((10,))] * 2
    scratch += [dma((4, 2, 3))] * 4 + [dma((2, 15))] * 2 + [dma((4, 2, 3))] * 4
    return pl.pallas_call(
        kernel,
        out_shape=jax.ShapeDtypeStruct((2, 8, D), BF),
        in_specs=[pl.BlockSpec(memory_space=pltpu.SMEM)] + [vmem] * 3 + [hbm] * 7,
        out_specs=vmem,
        scratch_shapes=scratch,
        compiler_params=pltpu.CompilerParams(
            collective_id=0, has_side_effects=True, vmem_limit_bytes=60 * 1024 * 1024
        ),
    )(lengths, inputs, cosine, sine, queries, cache, down_latent, value_up, output_weight, up_weight, down_weight)


def body(queries, latent_cache, lengths, inputs, down_latent, value_up, output_weight, up_weight, down_weight):
    frequency = ROPE_BASE ** (-jnp.arange(32, dtype=F32) / 32)
    position = jnp.concatenate([lengths, lengths + 1]).astype(F32)
    angles = position[:, None] * frequency[None, :]
    cosine, sine = jnp.cos(angles), jnp.sin(angles)
    return layer(
        lengths, inputs,
        jnp.concatenate([cosine, cosine], axis=-1), jnp.concatenate([-sine, sine], axis=-1),
        queries, latent_cache, down_latent, value_up, output_weight, up_weight, down_weight,
    )


def solution(mesh):
    return jax.shard_map(
        body,
        mesh=mesh,
        in_specs=(
            P(None, ("dp", "tp"), None, None),
            P(("dp", "tp"), None, None),
            P(("dp", "tp")),
            P(None, ("dp", "tp"), None),
            P("tp", None),
            P("tp", None, None),
            P("tp", "dp"),
            P(None, "tp"),
            P("tp", None),
        ),
        out_specs=P(None, ("dp", "tp"), None),
        check_vma=False,
    )
```

time: 639 us -> 123 us (0.19)
  waiting for transfers between devices: 495 us -> 0 us
  Pallas kernels: 0 us -> 104 us
  blocking collectives: 67.5 us -> 0 us
  matrix products: 46.7 us -> 0 us
  between operations: 15.9 us -> 0.02 us
  local copies, waits for them, and re-layouts: 2.5 us -> 15.5 us
  other arithmetic: 10.4 us -> 2.2 us
    unnamed x13 -> x0, waiting for transfers between devices: 417 us -> none
    pallas_call x0 -> x1, Pallas kernels: none -> 104 us  [layer(): pl.pallas_call(kernel, out_shape=jax.ShapeDtypeStruct((2, 8, D), BF), in_...]
    all_gather x3 -> x0, waiting for transfers between devices: 78.5 us -> none  [the longest x2 78.4 us: body(): lax.all_gather(ffn_input, 'tp', axis=0, tiled=True)]
    all_to_all x4 -> x0, blocking collectives: 67.5 us -> none  [the longest x2 39.8 us: body(): lax.all_to_all(attended, 'tp', split_axis=1, concat_axis=0, tiled=True)]
    dot_general x15 -> x0, matrix products: 46.7 us -> none  [the longest x2 14.4 us: body(): jnp.dot(activation, down_weight, preferred_element_type=jnp.float32)]
    unnamed x21 -> x4, local copies, waits for them, and re-layouts: 1.28 us -> 15.5 us
  transfers between devices with their start and end apart: 8 -> 0, of which waited for: 7 -> 0; matrix products, arithmetic and copies ran while one was open for 4% -> 0% of each run, Pallas kernels for 0% -> 0%
where the time goes in v1:
time: 123 us; the launch traced here: 122 us
  Pallas kernels  104 us (85%)
  local copies, waits for them, and re-layouts  15.5 us (13%)
  other arithmetic  2.2 us (2%)
    pallas_call x1, Pallas kernels, layer(): pl.pallas_call(kernel, out_shape=jax.ShapeDtypeStruct((2, 8, D), BF), in_...  104 us
    unnamed x4, local copies, waits for them, and re-layouts  15.5 us

profile of v1, /device:TPU:0, one launch (start us, length us, event | category | flops | bytes accessed | tf_op | source)
XLA Modules:
  0.0 122.2 jit_solution(17311862183600745605)
XLA Ops:
  0.0 0.7 broadcast_add_fusion
  0.7 0.7 add_convert_fusion
  1.4 0.1 fusion
  1.5 0.7 pad_maximum_fusion
  2.2 1.9 %copy.12.dl_hbm = bf16[256,576]{1,0:T(8,128)(2,1)} copy(bf16[256,576]{0,1:T(8,128)(2,1)} %param.13) | data formatting | bytes 589824 | tf_op args[4]
  4.1 4.3 %copy.10.q_hbm = bf16[2,8,128,576]{3,2,1,0:T(8,128)(2,1)} copy(bf16[2,8,128,576]{2,3,1,0:T(8,128)(2,1)} %param.9) | data formatting | bytes 4718592 | tf_op args[0]
  8.4 7.7 %copy.11.c_hbm = bf16[8,512,576]{2,1,0:T(8,128)(2,1)} copy(bf16[8,512,576]{1,2,0:T(8,128)(2,1)} %param.10) | data formatting | bytes 9437184 | tf_op args[1]
  16.1 104.5 %shard_map.91 = bf16[2,8,4096]{2,1,0:T(8,128)(2,1)} custom-call(s32[8]{0:T(128)} %lens.1, bf16[2,8,4096]{2,1,0:T(8,128)(2,1)} %x_in.1, f32[16,64]{1,0:T(8,128)} %get-tuple-element.8.cos_in, f32[16,64]{1,0:T(8,128)} %get-tuple-element.9.sin_in, bf16[2,8,128,576]{3,2,1,0:T(8,128)(2,1)} %copy.10.q_hbm, bf16[8,512,576]{2,1,0:T(8,128)(2,1)} %copy.11.c_hbm, ...), custom_call_target="tpu_custom_call" | custom-call | tf_op jit(solution)/shard_map/pallas_call | solution.py:478
  120.6 1.6 %copy.14 = bf16[2,8,4096]{2,1,0:T(8,128)(2,1)} copy(bf16[2,8,4096]{2,1,0:T(8,128)(2,1)} %shard_map.91) | data formatting | bytes 262144
  (1 shorter events, 0.0 us)

commit v2 on v0

v2 whole, which is shorter than its diff:
```python
import math

import jax
import jax.numpy as jnp
import numpy as np
from jax import lax
from jax.experimental import pallas as pl
from jax.experimental.pallas import tpu as pltpu
from jax.sharding import PartitionSpec as P

LAT = 512
WIDTH = 576
CTX = 512
D = 4096
FF = 640
EPSILON = 1e-06
SCORE_SCALE = 192.0 ** (-0.5)
ROPE_BASE = 10000.0
NEG = -1e30
BF = jnp.bfloat16
F32 = jnp.float32
MESH = pl.DeviceIdType.MESH

PLANE = (
    (0, 1), (0, 3), (1, 0), (3, 0), (2, 1), (1, 2), (2, 3), (3, 2),
    (2, 2), (1, 1), (3, 3), (1, 3), (3, 1), (0, 2), (2, 0),
)
LINE = (1, 3, 2)


def copy_to(src, dst, send_sem, recv_sem, device):
    return pltpu.make_async_remote_copy(
        src_ref=src, dst_ref=dst, send_sem=send_sem, recv_sem=recv_sem,
        device_id=device, device_id_type=MESH,
    )


def cos_sin(angles):
    turns = jnp.floor(angles * (0.5 / np.pi) + 0.5)
    rest = angles - turns * 6.28125
    rest = rest - turns * (2 * np.pi - 6.28125)
    square = rest * rest
    cosine = jnp.zeros_like(square)
    sine = jnp.zeros_like(square)
    for n in range(8, -1, -1):
        cosine = cosine * square + (-1.0) ** n / math.factorial(2 * n)
        sine = sine * square + (-1.0) ** n / math.factorial(2 * n + 1)
    return cosine, sine * rest


def kernel(
    lens, x_hbm, freq_hbm, q_hbm, c_hbm, dl_hbm, vu_hbm, ow_hbm, up_hbm, dn_hbm,
    out,
    x_in, freq_in, q_v, c_v, dl_v, vu_v, w_v, up_v, dn_v,
    xr, ps, pr, keys_b, keys_f, o_v, m_v, l_v,
    send_a, recv_a, val_f, val_b, hid, acc, square, act,
    mix_s, mix_r, key_s, key_r, keep_f, fresh_f,
    c_send1, c_recv1, c_send2, c_recv2, gath, c_tail1, c_tail2, c_tail3, c_tail4, gath_tail,
    e_send1, e_recv1, e_send2, e_recv2, e_tail1, e_tail2, e_tail3, e_tail4,
    sem_q, sem_c, sem_w, sem_vu,
    ss_x, rs_x, ss_p, rs_p, ss_a, rs_a, ss_m, rs_m, ss_k, rs_k, ss_w, rs_w, ss_g, rs_g,
    ss_c1, rs_c1, ss_c2, rs_c2, ss_e1, rs_e1, ss_e2, rs_e2,
):
    dp = lax.axis_index("dp")
    tp = lax.axis_index("tp")
    y, core = dp // 2, dp % 2
    z, x = tp // 4, tp % 4
    plane = [((z + dz) % 4) * 4 + (x + dx) % 4 for dz, dx in PLANE]
    on_x = {k: (dp, z * 4 + (x + k) % 4) for k in LINE}
    on_z = {k: (dp, ((z + k) % 4) * 4 + x) for k in LINE}
    y_up, y_dn, y_far = (y + 1) % 4, (y + 3) % 4, (y + 2) % 4
    sibling = y * 2 + 1 - core

    barrier = pltpu.get_barrier_semaphore()
    partners = [(dp, t) for t in plane] + [
        (sibling, tp), (y_up * 2 + core, tp), (y_dn * 2 + core, tp)
    ]
    for device in partners:
        pl.semaphore_signal(barrier, inc=1, device_id=device, device_id_type=MESH)

    def q_copy(r):
        return pltpu.make_async_copy(q_hbm.at[:, r], q_v.at[:, r], sem_q.at[r])

    def c_copy(r):
        return pltpu.make_async_copy(c_hbm.at[r], c_v.at[r], sem_c.at[r])

    dl_copy = pltpu.make_async_copy(dl_hbm, dl_v, sem_w.at[0])
    ow_copy = pltpu.make_async_copy(ow_hbm, w_v.at[dp], sem_w.at[1])
    up_copy = pltpu.make_async_copy(up_hbm, up_v, sem_w.at[2])
    dn_copy = pltpu.make_async_copy(dn_hbm, dn_v, sem_w.at[3])
    x_copy = pltpu.make_async_copy(x_hbm, x_in, sem_w.at[4])
    freq_copy = pltpu.make_async_copy(freq_hbm, freq_in, sem_w.at[5])
    vu_copies = [
        pltpu.make_async_copy(vu_hbm.at[h], vu_v.at[:, pl.ds(h * 128, 128)], sem_vu.at[h])
        for h in range(8)
    ]
    x_copy.start()
    for r in range(8):
        q_copy(r).start()
        c_copy(r).start()
        if r == 1:
            dl_copy.start()
            freq_copy.start()

    pl.semaphore_wait(barrier, len(partners))

    def x_slice(t):
        return x_hbm.at[:, :, pl.ds(pl.multiple_of(t * 256, 256), 256)]

    x_copies = [
        copy_to(x_slice(t), xr.at[tp], ss_x.at[k], rs_x.at[k], (dp, t))
        for k, t in enumerate(plane)
    ]
    for c in x_copies:
        c.start()
    x_own = pltpu.make_async_copy(x_slice(tp), xr.at[tp], sem_w.at[6])
    x_own.start()

    lo, hi = pl.ds(0, 512), pl.ds(512, 512)
    up_dev, dn_dev, sib_dev = (y_up * 2 + core, tp), (y_dn * 2 + core, tp), (sibling, tp)
    w_up = [
        copy_to(ow_hbm.at[s], w_v.at[dp, s], ss_w.at[i], rs_w.at[i], up_dev)
        for i, s in enumerate((lo, hi))
    ]
    w_dn = [
        copy_to(ow_hbm.at[s], w_v.at[dp, s], ss_w.at[2 + i], rs_w.at[2 + i], dn_dev)
        for i, s in enumerate((hi, lo))
    ]
    w_sib = copy_to(ow_hbm, w_v.at[dp], ss_w.at[4], rs_w.at[4], sib_dev)
    from_dn, from_up, from_far = y_dn * 2 + core, y_up * 2 + core, y_far * 2 + core
    w_up2 = copy_to(w_v.at[from_dn, lo], w_v.at[from_dn, lo], ss_w.at[5], rs_w.at[5], up_dev)
    w_dn2 = copy_to(w_v.at[from_up, hi], w_v.at[from_up, hi], ss_w.at[6], rs_w.at[6], dn_dev)
    w_sib_dn = copy_to(w_v.at[from_dn], w_v.at[from_dn], ss_w.at[7], rs_w.at[7], sib_dev)
    w_sib_up = copy_to(w_v.at[from_up], w_v.at[from_up], ss_w.at[8], rs_w.at[8], sib_dev)
    w_sib_far = copy_to(w_v.at[from_far], w_v.at[from_far], ss_w.at[9], rs_w.at[9], sib_dev)
    for c in (w_up[0], w_dn[0], w_up[1], w_dn[1], w_sib):
        c.start()
    ow_copy.start()

    def a_copies(step, g):
        rows = pl.ds(2 * g, 2)
        return [
            copy_to(send_a.at[step, rows, t], recv_a.at[step, rows, tp],
                    ss_a.at[step, g, k], rs_a.at[step, g, k], (dp, t))
            for k, t in enumerate(plane)
        ]

    def attend_row(r):
        q_copy(r).wait()
        c_copy(r).wait()
        q = jnp.concatenate([q_v[0, r], q_v[1, r]], axis=1)
        k = c_v[r]
        s = lax.dot_general(
            q, k, (((0,), (0,)), ((), ())), preferred_element_type=F32
        ) * SCORE_SCALE
        position = lax.broadcasted_iota(jnp.int32, (1, CTX), 1)
        s = jnp.where(position < lens[r], s, NEG)
        m = jnp.max(s, axis=-1, keepdims=True)
        p = jnp.exp(s - m)
        total = jnp.sum(p, axis=-1, keepdims=True)
        l_v[r] = total
        m_v[r] = m
        o = lax.dot_general(
            p.astype(BF), k[:LAT], (((1,), (1,)), ((), ())), preferred_element_type=F32
        )
        o_v[r] = o[128:]
        return (o[:128] * (1.0 / total[:128])).reshape(16, 8, LAT)

    def attend_pair(pair, carry):
        both = [attend_row(2 * pair), attend_row(2 * pair + 1)]
        send_a[0, pair] = jnp.concatenate(both, axis=1).astype(BF)
        recv_a[0, pair, tp] = send_a[0, pair, tp]
        return carry

    lax.fori_loop(0, 1, attend_pair, 0)

    for c in vu_copies:
        c.start()
    up_copy.start()
    dn_copy.start()

    dl_copy.wait()
    x_own.wait()
    for c in x_copies:
        c.wait_recv()
    partial = lax.dot_general(
        xr[...].astype(F32).reshape(256, 256).astype(BF), dl_v[...], (((1,), (1,)), ((), ())),
        preferred_element_type=F32,
    )
    ps[...] = partial.astype(BF).reshape(16, 16, WIDTH)
    p_copies = [
        copy_to(ps.at[t], pr.at[k], ss_p.at[k], rs_p.at[k], (dp, t))
        for k, t in enumerate(plane)
    ]
    for c in p_copies:
        c.start()

    def attend_and_send(pair, carry):
        attend_pair(pair, carry)

        @pl.when(pair % 2 == 1)
        def _():
            for c in a_copies(0, pair // 2):
                c.start()

        return carry

    lax.fori_loop(1, 4, attend_and_send, 0)

    freq_copy.wait()
    x_copy.wait()
    x0 = jnp.concatenate([x_in[0].astype(F32), x_in[1].astype(F32)], axis=0)
    x_scale = lax.rsqrt(jnp.mean(x0 * x0, axis=-1, keepdims=True) + EPSILON)
    for c in p_copies:
        c.wait_recv()
    comp = ps[tp].astype(F32)
    for k in range(15):
        comp = comp + pr[k].astype(F32)
    comp = comp * x_scale
    lat = comp[:, :LAT]
    lat = lat * lax.rsqrt(jnp.mean(lat * lat, axis=-1, keepdims=True) + EPSILON)
    rope = comp[:, LAT:]
    swapped = jnp.concatenate([rope[:, 32:], rope[:, :32]], axis=-1)
    row = lax.broadcasted_iota(jnp.int32, (16, 64), 0)
    position = row // 8
    for r in range(8):
        position = position + jnp.where(row % 8 == r, lens[r], 0)
    cosine, sine = cos_sin(position.astype(F32) * freq_in[...])
    first = lax.broadcasted_iota(jnp.int32, (16, 64), 1) < 32
    rotated = rope * cosine + swapped * jnp.where(first, -sine, sine)
    keys_b[:, :LAT] = lat.astype(BF)
    keys_b[:, LAT:] = rotated.astype(BF)
    keys_f[...] = lat.astype(BF).astype(F32)

    key_s[...] = jnp.concatenate([lat[:8, :256], lat[:8, 256:]], axis=0).astype(BF)
    key_r[tp] = key_s[...]
    k_copies = [
        copy_to(key_s, key_r.at[tp], ss_k.at[k], rs_k.at[k], (dp, t)) for k, t in enumerate(plane)
    ]
    for c in k_copies:
        c.start()

    def fresh_scores(step, r):
        fresh = jnp.dot(keys_b[...], q_v[step, r], preferred_element_type=F32).T * SCORE_SCALE
        lane = lax.broadcasted_iota(jnp.int32, (128, 16), 1)
        s0 = jnp.sum(jnp.where(lane == r, fresh, 0.0), axis=-1, keepdims=True)
        s1 = jnp.sum(jnp.where(lane == r + 8, fresh, 0.0), axis=-1, keepdims=True)
        return s0, s1

    def mix_row(r, mix):
        s0, _ = fresh_scores(0, r)
        m_old = m_v[r, :128]
        m = jnp.maximum(m_old, s0)
        cached = jnp.exp(m_old - m) * l_v[r, :128]
        p0 = jnp.exp(s0 - m)
        inverse = 1.0 / (cached + p0)
        lane = lax.broadcasted_iota(jnp.int32, (128, 128), 1)
        mix = jnp.where(lane == r, cached * inverse, mix)
        return jnp.where(lane == r + 8, p0 * inverse, mix)

    mix = lax.fori_loop(0, 8, mix_row, jnp.zeros((128, 128), F32))
    mix_s[...] = mix.reshape(16, 8, 128)
    mix_r[tp] = mix_s[tp]
    m_copies = [
        copy_to(mix_s.at[t], mix_r.at[tp], ss_m.at[k], rs_m.at[k], (dp, t))
        for k, t in enumerate(plane)
    ]
    for c in m_copies:
        c.start()

    def finish_row(r):
        s0, s1 = fresh_scores(1, r)
        m_old = m_v[r, 128:]
        m = jnp.maximum(jnp.maximum(m_old, s0), s1)
        keep = jnp.exp(m_old - m)
        p0 = jnp.exp(s0 - m)
        p1 = jnp.exp(s1 - m)
        inverse = 1.0 / (keep * l_v[r, 128:] + p0 + p1)
        k0 = keys_f[pl.ds(r, 1), :]
        k1 = keys_f[pl.ds(r + 8, 1), :]
        o = o_v[r] * (keep * inverse) + (p0 * inverse) * k0 + (p1 * inverse) * k1
        return o.reshape(16, 8, LAT)

    def finish_four(g, carry):
        for j in range(2):
            pair = 2 * g + j
            both = [finish_row(2 * pair), finish_row(2 * pair + 1)]
            send_a[1, pair] = jnp.concatenate(both, axis=1).astype(BF)
            recv_a[1, pair, tp] = send_a[1, pair, tp]
        for c in a_copies(1, g):
            c.start()
        return carry

    lax.fori_loop(0, 2, finish_four, 0)

    def values(step):
        def four(g, carry):
            for c in a_copies(step, g):
                c.wait_recv()
            head = lax.broadcasted_iota(jnp.int32, (8, 128), 0)[None]
            for j in range(2):
                pair = 2 * g + j
                a = recv_a[step, pair].reshape(256, LAT)
                full = jnp.dot(a, vu_v[...], preferred_element_type=F32)
                full = full.reshape(32, 8, 1024)
                own = jnp.where(head == 0, full[:, :, :128], 0.0)
                for h in range(1, 8):
                    own = jnp.where(head == h, full[:, :, h * 128:(h + 1) * 128], own)
                for b in range(32):
                    at = pl.multiple_of((b // 2) * 64 + (2 * pair + b % 2) * 8, 8)
                    val_f[pl.ds(at, 8), :] = own[b]
            return carry

        lax.fori_loop(0, 2, four, 0)
        if step == 0:
            for c in k_copies + m_copies:
                c.wait_recv()

            def spread(src, carry):
                tile = mix_r[src]
                for r in range(8):
                    at = pl.ds(pl.multiple_of(src * 64 + r * 8, 8), 8)
                    keep_f[at, :] = jnp.broadcast_to(tile[:, r:r + 1], (8, 128))
                    fresh_f[at, :] = jnp.broadcast_to(tile[:, r + 8:r + 9], (8, 128))
                return carry

            lax.fori_loop(0, 16, spread, 0)
            keys = key_r[...].astype(F32)
            keys = jnp.concatenate([keys[:, :8], keys[:, 8:]], axis=2).reshape(128, LAT).astype(BF)
            projected = jnp.dot(keys, vu_v[...], preferred_element_type=F32)
        for h in range(8):
            cols = slice(h * 128, (h + 1) * 128)
            own = pl.ds(h, 128, stride=8)
            if step == 0:
                mixed = keep_f[own, :] * val_f[own, :] + fresh_f[own, :] * projected[:, cols]
                val_b[0, :, cols] = mixed.astype(BF)
            else:
                val_b[1, :, cols] = val_f[own, :].astype(BF)

    def ways(order):
        return ((order[0:3], order[3:6]), (order[6:7], order[7:8]))

    c_cols = ways([b * 2 + c for b in (y, y_up, y_dn, y_far) for c in range(2)])
    e_cols = ways(list(range(8)))

    def fold(a):
        return jnp.concatenate([a[..., :256], a[..., 256:]], axis=-2)

    def unfold(a):
        return jnp.concatenate([a[..., :8, :], a[..., 8:, :]], axis=-1)

    class Sum:
        def __init__(self, cols, parts, sems):
            self.cols, self.parts = cols, parts
            self.ss1, self.rs1, self.ss2, self.rs2 = sems

        def share(self, step, i, way, k):
            send1 = self.parts[i][0]
            if way == 0:
                return send1.at[step, 0, :, (x + k) % 4]
            return send1.at[step, 1, (z + k) % 4]

        def first(self, step, i, way, n):
            on = on_x if way == 0 else on_z
            k = LINE[n]
            return copy_to(self.share(step, i, way, k), self.parts[i][1].at[step, way, n],
                           self.ss1.at[step, i, way, n], self.rs1.at[step, i, way, n], on[k])

        def last(self, step, i, way, n):
            on, here = (on_z, z) if way == 0 else (on_x, x)
            k = LINE[n]
            return copy_to(self.parts[i][2].at[step, way, (here + k) % 4], self.parts[i][3].at[step, way, n],
                           self.ss2.at[step, i, way, n], self.rs2.at[step, i, way, n], on[k])

        def begin(self, step, i, multiply):
            for way in range(2):
                for m, col in enumerate(self.cols[i][way]):
                    block = fold(multiply(col).reshape(16, 8, 512)).astype(BF)
                    self.parts[i][0][step, way, :, :, :, m * 256:(m + 1) * 256] = block.reshape(4, 4, 16, 256)
                for n in range(3):
                    self.first(step, i, way, n).start()

        def middle(self, step, i):
            for way in range(2):
                total = self.share(step, i, way, 0)[...].astype(F32)
                for n in range(3):
                    self.first(step, i, way, n).wait_recv()
                    total = total + self.parts[i][1][step, way, n].astype(F32)
                self.parts[i][2][step, way] = total.astype(BF)
                for n in range(3):
                    self.last(step, i, way, n).start()

        def end(self, step, i, way):
            total = self.parts[i][2][step, way, z if way == 0 else x].astype(F32)
            for n in range(3):
                self.last(step, i, way, n).wait_recv()
                total = total + self.parts[i][3][step, way, n].astype(F32)
            return total

        def drain(self):
            for step in range(2):
                for i in range(2):
                    for way in range(2):
                        for n in range(3):
                            self.first(step, i, way, n).wait_send()
                            self.last(step, i, way, n).wait_send()

    c_sum = Sum(
        c_cols,
        ((c_send1, c_recv1, c_send2, c_recv2), (c_tail1, c_tail2, c_tail3, c_tail4)),
        (ss_c1, rs_c1, ss_c2, rs_c2),
    )
    e_sum = Sum(
        e_cols,
        ((e_send1, e_recv1, e_send2, e_recv2), (e_tail1, e_tail2, e_tail3, e_tail4)),
        (ss_e1, rs_e1, ss_e2, rs_e2),
    )

    def begin_c(step, i):
        c_sum.begin(step, i, lambda col: jnp.dot(
            val_b[step], w_v[col], preferred_element_type=F32
        ))

    rows_in = (gath, gath_tail)

    def g_first(step, i, way, n):
        on = on_x if way == 0 else on_z
        block = rows_in[i].at[step, way, z, x]
        return copy_to(block, block, ss_g.at[step, i, way, n], rs_g.at[step, i, way, n], on[LINE[n]])

    def g_last(step, i, way, n):
        on = on_z if way == 0 else on_x
        block = rows_in[i].at[step, 0, z] if way == 0 else rows_in[i].at[step, 1, :, x]
        return copy_to(block, block, ss_g.at[step, i, way, 3 + n], rs_g.at[step, i, way, 3 + n], on[LINE[n]])

    def hidden(step, i):
        for way in range(2):
            total = c_sum.end(step, i, way)
            for m, col in enumerate(c_cols[i][way]):
                own = x_in[step, :, pl.ds(pl.multiple_of(col * 512, 512), 512)].astype(F32)
                here = slice(m * 256, (m + 1) * 256)
                block = total[:, here] + fold(own)
                hid[step, col] = block
                rows_in[i][step, way, z, x, :, here] = block.astype(BF)
            for n in range(3):
                g_first(step, i, way, n).start()

    def gather(step, i):
        for way in range(2):
            for n in range(3):
                g_first(step, i, way, n).wait_recv()
            for n in range(3):
                g_last(step, i, way, n).start()

    def expand(step, i):
        total = None
        squares = None
        for way in range(2):
            for n in range(3):
                g_last(step, i, way, n).wait_recv()
            for m, col in enumerate(c_cols[i][way]):
                rows = rows_in[i][step, way, :, :, :, m * 256:(m + 1) * 256].reshape(16, 16, 256)
                a = unfold(rows.astype(F32)).reshape(128, 512)
                more = jnp.sum(a * a, axis=-1, keepdims=True)
                term = jnp.dot(a.astype(BF), up_v[col], preferred_element_type=F32)
                total = term if total is None else total + term
                squares = more if squares is None else squares + more
        if i == 0:
            acc[step] = total
            square[step] = squares
        else:
            v = (acc[step] + total) * lax.rsqrt((square[step] + squares) / D + EPSILON)
            act[step] = (v / (1.0 + jnp.exp(-v))).astype(BF)

    def begin_e(step, i):
        e_sum.begin(step, i, lambda col: jnp.dot(
            act[step], dn_v[:, col * 512:(col + 1) * 512], preferred_element_type=F32
        ))

    def finish(step, i):
        for way in range(2):
            total = e_sum.end(step, i, way)
            for m, col in enumerate(e_cols[i][way]):
                result = unfold(hid[step, col] + total[:, m * 256:(m + 1) * 256])
                out[step, :, col * 512:(col + 1) * 512] = result.astype(BF)

    def weights_near():
        w_up[1].wait_recv()
        w_dn[1].wait_recv()
        w_sib_up.start()
        w_sib_dn.start()
        ow_copy.wait()
        w_sib.wait_recv()
        w_sib_up.wait_recv()
        w_sib_dn.wait_recv()

    def weights_far():
        w_up2.wait_recv()
        w_dn2.wait_recv()
        w_sib_far.start()
        w_sib_far.wait_recv()

    w_up[0].wait_recv()
    w_up2.start()
    w_dn[0].wait_recv()
    w_dn2.start()
    for c in vu_copies:
        c.wait()
    values(0)
    weights_near()
    begin_c(0, 0)
    values(1)
    begin_c(1, 0)
    c_sum.middle(0, 0)
    weights_far()
    begin_c(0, 1)
    begin_c(1, 1)
    c_sum.middle(1, 0)
    hidden(0, 0)
    c_sum.middle(0, 1)
    c_sum.middle(1, 1)
    hidden(1, 0)
    hidden(0, 1)
    gather(0, 0)
    gather(0, 1)
    hidden(1, 1)
    gather(1, 0)
    up_copy.wait()
    expand(0, 0)
    gather(1, 1)
    expand(0, 1)
    dn_copy.wait()
    begin_e(0, 0)
    expand(1, 0)
    begin_e(0, 1)
    expand(1, 1)
    begin_e(1, 0)
    begin_e(1, 1)
    e_sum.middle(0, 0)
    e_sum.middle(0, 1)
    e_sum.middle(1, 0)
    e_sum.middle(1, 1)
    finish(0, 0)
    finish(0, 1)
    finish(1, 0)
    finish(1, 1)

    for c in x_copies + p_copies + k_copies + m_copies:
        c.wait_send()

    def drain(i, carry):
        for c in a_copies(i // 2, i % 2):
            c.wait_send()
        return carry

    lax.fori_loop(0, 4, drain, 0)
    for c in w_up + w_dn + [w_sib, w_up2, w_dn2, w_sib_dn, w_sib_up, w_sib_far]:
        c.wait_send()
    c_sum.drain()
    e_sum.drain()
    for step in range(2):
        for i in range(2):
            for way in range(2):
                for n in range(3):
                    g_first(step, i, way, n).wait_send()
                    g_last(step, i, way, n).wait_send()


def layer(lengths, inputs, frequency, queries, cache, down_latent, value_up, output_weight, up_weight, down_weight):
    vmem, hbm = pl.BlockSpec(memory_space=pltpu.VMEM), pl.BlockSpec(memory_space=pl.ANY)
    dma = pltpu.SemaphoreType.DMA
    scratch = [
        pltpu.VMEM((2, 8, D), BF),
        pltpu.VMEM((16, 64), F32),
        pltpu.VMEM((2, 8, WIDTH, 128), BF),
        pltpu.VMEM((8, WIDTH, CTX), BF),
        pltpu.VMEM((WIDTH, 256), BF),
        pltpu.VMEM((LAT, 1024), BF),
        pltpu.VMEM((8, 1024, 512), BF),
        pltpu.VMEM((8, 512, FF), BF),
        pltpu.VMEM((FF, D), BF),
        pltpu.VMEM((16, 2, 8, 256), BF),
        pltpu.VMEM((16, 16, WIDTH), BF),
        pltpu.VMEM((15, 16, WIDTH), BF),
        pltpu.VMEM((16, WIDTH), BF),
        pltpu.VMEM((16, LAT), F32),
        pltpu.VMEM((8, 128, LAT), F32),
        pltpu.VMEM((8, 256, 1), F32),
        pltpu.VMEM((8, 256, 1), F32),
        pltpu.VMEM((2, 4, 16, 16, LAT), BF),
        pltpu.VMEM((2, 4, 16, 16, LAT), BF),
        pltpu.VMEM((1024, 128), F32),
        pltpu.VMEM((2, 128, 1024), BF),
        pltpu.VMEM((2, 8, 16, 256), F32),
        pltpu.VMEM((2, 128, FF), F32),
        pltpu.VMEM((2, 128, 1), F32),
        pltpu.VMEM((2, 128, FF), BF),
    ]
    scratch += [
        pltpu.VMEM((16, 8, 128), F32),
        pltpu.VMEM((16, 8, 128), F32),
        pltpu.VMEM((16, 256), BF),
        pltpu.VMEM((16, 16, 256), BF),
        pltpu.VMEM((1024, 128), F32),
        pltpu.VMEM((1024, 128), F32),
    ]
    for gathers in (1, 0):
        for width in (768, 256):
            scratch += [
                pltpu.VMEM((2, 2, 4, 4, 16, width), BF),
                pltpu.VMEM((2, 2, 3, 4, 16, width), BF),
                pltpu.VMEM((2, 2, 4, 16, width), BF),
                pltpu.VMEM((2, 2, 3, 16, width), BF),
            ] + [pltpu.VMEM((2, 2, 4, 4, 16, width), BF)] * gathers
    scratch += [dma((8,)), dma((8,)), dma((7,)), dma((8,))]
    scratch += [dma((15,))] * 4 + [dma((2, 2, 15))] * 2 + [dma((15,))] * 4 + [dma((10,))] * 2 + [dma((2, 2, 2, 6))] * 2
    scratch += [dma((2, 2, 2, 3))] * 8
    return pl.pallas_call(
        kernel,
        out_shape=jax.ShapeDtypeStruct((2, 8, D), BF),
        in_specs=[pl.BlockSpec(memory_space=pltpu.SMEM)] + [hbm] * 9,
        out_specs=vmem,
        scratch_shapes=scratch,
        compiler_params=pltpu.CompilerParams(
            collective_id=0, has_side_effects=True, vmem_limit_bytes=60 * 1024 * 1024
        ),
    )(lengths, inputs, frequency, queries, cache, down_latent, value_up, output_weight, up_weight, down_weight)


def body(queries, latent_cache, lengths, inputs, down_latent, value_up, output_weight, up_weight, down_weight):
    half = ROPE_BASE ** (-np.arange(32, dtype=np.float32) / np.float32(32))
    frequency = np.tile(half.astype(np.float32), (16, 2))
    return layer(
        lengths, inputs, jnp.asarray(frequency),
        jnp.swapaxes(queries, 2, 3), jnp.swapaxes(latent_cache, 1, 2), down_latent.T,
        value_up, output_weight, up_weight.reshape(8, 512, FF), down_weight,
    )


def solution(mesh):
    return jax.shard_map(
        body,
        mesh=mesh,
        in_specs=(
            P(None, ("dp", "tp"), None, None),
            P(("dp", "tp"), None, None),
            P(("dp", "tp")),
            P(None, ("dp", "tp"), None),
            P("tp", None),
            P("tp", None, None),
            P("tp", "dp"),
            P(None, "tp"),
            P("tp", None),
        ),
        out_specs=P(None, ("dp", "tp"), None),
        check_vma=False,
    )
```

time: 639 us -> 96.5 us (0.15)
  waiting for transfers between devices: 495 us -> 0 us
  Pallas kernels: 0 us -> 94.3 us
  blocking collectives: 67.5 us -> 0 us
  matrix products: 46.7 us -> 0 us
  between operations: 15.9 us -> 0.01 us
  other arithmetic: 10.4 us -> 0 us
    unnamed x13 -> x0, waiting for transfers between devices: 417 us -> none
    pallas_call x0 -> x1, Pallas kernels: none -> 94.3 us  [layer(): pl.pallas_call(kernel, out_shape=jax.ShapeDtypeStruct((2, 8, D), BF), in_...]
    all_gather x3 -> x0, waiting for transfers between devices: 78.5 us -> none  [the longest x2 78.4 us: body(): lax.all_gather(ffn_input, 'tp', axis=0, tiled=True)]
    all_to_all x4 -> x0, blocking collectives: 67.5 us -> none  [the longest x2 39.8 us: body(): lax.all_to_all(attended, 'tp', split_axis=1, concat_axis=0, tiled=True)]
    dot_general x15 -> x0, matrix products: 46.7 us -> none  [the longest x2 14.4 us: body(): jnp.dot(activation, down_weight, preferred_element_type=jnp.float32)]
  transfers between devices with their start and end apart: 8 -> 0, of which waited for: 7 -> 0; matrix products, arithmetic and copies ran while one was open for 4% -> 0% of each run, Pallas kernels for 0% -> 0%
where the time goes in v2:
time: 96.5 us; the launch traced here: 95.9 us
  Pallas kernels  94.3 us (98%)
  local copies, waits for them, and re-layouts  1.57 us (2%)
    pallas_call x1, Pallas kernels, layer(): pl.pallas_call(kernel, out_shape=jax.ShapeDtypeStruct((2, 8, D), BF), in_...  94.3 us

profile of v2, /device:TPU:0, one launch (start us, length us, event | category | flops | bytes accessed | tf_op | source)
XLA Modules:
  0.0 95.9 jit_solution(13370504907007958293)
XLA Ops:
  0.0 94.3 %shard_map.100 = bf16[2,8,4096]{2,1,0:T(8,128)(2,1)} custom-call(s32[8]{0:T(128)} %lens.1, bf16[2,8,4096]{2,1,0:T(8,128)(2,1)} %x_hbm.1, f32[16,64]{1,0:T(8,128)} %constant.2.clone.freq_hbm, bf16[2,8,576,128]{3,2,1,0:T(8,128)(2,1)} %bitcast.6, bf16[8,576,512]{2,1,0:T(8,128)(2,1)} %bitcast.5, bf16[576,256]{1,0:T(8,128)(2,1)} %bitcast.7, ...), custom_call_target="tpu_custom_call" | custom-call | tf_op jit(solution)/shard_map/pallas_call | solution.py:618
  94.3 1.6 %copy.12 = bf16[2,8,4096]{2,1,0:T(8,128)(2,1)} copy(bf16[2,8,4096]{2,1,0:T(8,128)(2,1)} %shard_map.100) | data formatting | bytes 262144

commit v3 on v2

--- a/solution.py
+++ b/solution.py
@@ -33,6 +33,10 @@
         src_ref=src, dst_ref=dst, send_sem=send_sem, recv_sem=recv_sem,
         device_id=device, device_id_type=MESH,
     )
+
+
+def all_of(region, send_sem, recv_sem, device):
+    return copy_to(region, region, send_sem, recv_sem, device)
 
 
 def cos_sin(angles):
@@ -68,6 +72,7 @@
     plane = [((z + dz) % 4) * 4 + (x + dx) % 4 for dz, dx in PLANE]
     on_x = {k: (dp, z * 4 + (x + k) % 4) for k in LINE}
     on_z = {k: (dp, ((z + k) % 4) * 4 + x) for k in LINE}
+    next_device = (dp, plane[0])
     y_up, y_dn, y_far = (y + 1) % 4, (y + 3) % 4, (y + 2) % 4
     sibling = y * 2 + 1 - core
 
@@ -95,12 +100,10 @@
         for h in range(8)
     ]
     x_copy.start()
-    for r in range(8):
+    for r in range(2):
         q_copy(r).start()
         c_copy(r).start()
-        if r == 1:
-            dl_copy.start()
-            freq_copy.start()
+    dl_copy.start()
 
     pl.semaphore_wait(barrier, len(partners))
 
@@ -108,11 +111,16 @@
         return x_hbm.at[:, :, pl.ds(pl.multiple_of(t * 256, 256), 256)]
 
     x_copies = [
-        copy_to(x_slice(t), xr.at[tp], ss_x.at[k], rs_x.at[k], (dp, t))
+        copy_to(x_slice(t), xr.at[tp], ss_x, rs_x, (dp, t))
         for k, t in enumerate(plane)
     ]
     for c in x_copies:
         c.start()
+    x_all = all_of(xr.at[pl.ds(0, 15)], ss_x, rs_x, next_device)
+    for r in range(2, 8):
+        q_copy(r).start()
+        c_copy(r).start()
+    freq_copy.start()
     x_own = pltpu.make_async_copy(x_slice(tp), xr.at[tp], sem_w.at[6])
     x_own.start()
 
@@ -141,9 +149,20 @@
         rows = pl.ds(2 * g, 2)
         return [
             copy_to(send_a.at[step, rows, t], recv_a.at[step, rows, tp],
-                    ss_a.at[step, g, k], rs_a.at[step, g, k], (dp, t))
-            for k, t in enumerate(plane)
+                    ss_a.at[step, g], rs_a.at[step, g], (dp, t))
+            for t in plane
         ]
+
+    def a_pair(pair):
+        return [
+            copy_to(send_a.at[0, pair, t], recv_a.at[0, pair, tp],
+                    ss_a.at[0, pair // 2], rs_a.at[0, pair // 2], (dp, t))
+            for t in plane
+        ]
+
+    def a_all(step, g):
+        return all_of(recv_a.at[step, pl.ds(2 * g, 2), pl.ds(0, 15)],
+                      ss_a.at[step, g], rs_a.at[step, g], next_device)
 
     def attend_row(r):
         q_copy(r).wait()
@@ -181,28 +200,26 @@
 
     dl_copy.wait()
     x_own.wait()
-    for c in x_copies:
-        c.wait_recv()
+    x_all.wait_recv()
     partial = lax.dot_general(
         xr[...].astype(F32).reshape(256, 256).astype(BF), dl_v[...], (((1,), (1,)), ((), ())),
         preferred_element_type=F32,
     )
     ps[...] = partial.astype(BF).reshape(16, 16, WIDTH)
     p_copies = [
-        copy_to(ps.at[t], pr.at[k], ss_p.at[k], rs_p.at[k], (dp, t))
+        copy_to(ps.at[t], pr.at[k], ss_p, rs_p, (dp, t))
         for k, t in enumerate(plane)
     ]
     for c in p_copies:
         c.start()
+    p_all = all_of(pr, ss_p, rs_p, next_device)
+    for c in a_pair(0):
+        c.start()
 
     def attend_and_send(pair, carry):
         attend_pair(pair, carry)
-
-        @pl.when(pair % 2 == 1)
-        def _():
-            for c in a_copies(0, pair // 2):
-                c.start()
-
+        for c in a_pair(pair):
+            c.start()
         return carry
 
     lax.fori_loop(1, 4, attend_and_send, 0)
@@ -211,8 +228,7 @@
     x_copy.wait()
     x0 = jnp.concatenate([x_in[0].astype(F32), x_in[1].astype(F32)], axis=0)
     x_scale = lax.rsqrt(jnp.mean(x0 * x0, axis=-1, keepdims=True) + EPSILON)
-    for c in p_copies:
-        c.wait_recv()
+    p_all.wait_recv()
     comp = ps[tp].astype(F32)
     for k in range(15):
         comp = comp + pr[k].astype(F32)
@@ -235,10 +251,11 @@
     key_s[...] = jnp.concatenate([lat[:8, :256], lat[:8, 256:]], axis=0).astype(BF)
     key_r[tp] = key_s[...]
     k_copies = [
-        copy_to(key_s, key_r.at[tp], ss_k.at[k], rs_k.at[k], (dp, t)) for k, t in enumerate(plane)
+        copy_to(key_s, key_r.at[tp], ss_k, rs_k, (dp, t)) for k, t in enumerate(plane)
     ]
     for c in k_copies:
         c.start()
+    k_all = all_of(key_r.at[pl.ds(0, 15)], ss_k, rs_k, next_device)
 
     def fresh_scores(step, r):
         fresh = jnp.dot(keys_b[...], q_v[step, r], preferred_element_type=F32).T * SCORE_SCALE
@@ -262,11 +279,12 @@
     mix_s[...] = mix.reshape(16, 8, 128)
     mix_r[tp] = mix_s[tp]
     m_copies = [
-        copy_to(mix_s.at[t], mix_r.at[tp], ss_m.at[k], rs_m.at[k], (dp, t))
+        copy_to(mix_s.at[t], mix_r.at[tp], ss_m, rs_m, (dp, t))
         for k, t in enumerate(plane)
     ]
     for c in m_copies:
         c.start()
+    m_all = all_of(mix_r.at[pl.ds(0, 15)], ss_m, rs_m, next_device)
 
     def finish_row(r):
         s0, s1 = fresh_scores(1, r)
@@ -295,8 +313,7 @@
 
     def values(step):
         def four(g, carry):
-            for c in a_copies(step, g):
-                c.wait_recv()
+            a_all(step, g).wait_recv()
             head = lax.broadcasted_iota(jnp.int32, (8, 128), 0)[None]
             for j in range(2):
                 pair = 2 * g + j
@@ -313,8 +330,8 @@
 
         lax.fori_loop(0, 2, four, 0)
         if step == 0:
-            for c in k_copies + m_copies:
-                c.wait_recv()
+            k_all.wait_recv()
+            m_all.wait_recv()
 
             def spread(src, carry):
                 tile = mix_r[src]
@@ -364,13 +381,21 @@
             on = on_x if way == 0 else on_z
             k = LINE[n]
             return copy_to(self.share(step, i, way, k), self.parts[i][1].at[step, way, n],
-                           self.ss1.at[step, i, way, n], self.rs1.at[step, i, way, n], on[k])
+                           self.ss1.at[step, i, way], self.rs1.at[step, i, way], on[k])
 
         def last(self, step, i, way, n):
             on, here = (on_z, z) if way == 0 else (on_x, x)
             k = LINE[n]
             return copy_to(self.parts[i][2].at[step, way, (here + k) % 4], self.parts[i][3].at[step, way, n],
-                           self.ss2.at[step, i, way, n], self.rs2.at[step, i, way, n], on[k])
+                           self.ss2.at[step, i, way], self.rs2.at[step, i, way], on[k])
+
+        def first_all(self, step, i, way):
+            return all_of(self.parts[i][1].at[step, way], self.ss1.at[step, i, way],
+                          self.rs1.at[step, i, way], next_device)
+
+        def last_all(self, step, i, way):
+            return all_of(self.parts[i][3].at[step, way], self.ss2.at[step, i, way],
+                          self.rs2.at[step, i, way], next_device)
 
         def begin(self, step, i, multiply):
             for way in range(2):
@@ -382,18 +407,18 @@
 
         def middle(self, step, i):
             for way in range(2):
+                self.first_all(step, i, way).wait_recv()
                 total = self.share(step, i, way, 0)[...].astype(F32)
                 for n in range(3):
-                    self.first(step, i, way, n).wait_recv()
                     total = total + self.parts[i][1][step, way, n].astype(F32)
                 self.parts[i][2][step, way] = total.astype(BF)
                 for n in range(3):
                     self.last(step, i, way, n).start()
 
         def end(self, step, i, way):
+            self.last_all(step, i, way).wait_recv()
             total = self.parts[i][2][step, way, z if way == 0 else x].astype(F32)
             for n in range(3):
-                self.last(step, i, way, n).wait_recv()
                 total = total + self.parts[i][3][step, way, n].astype(F32)
             return total
 
@@ -401,9 +426,8 @@
             for step in range(2):
                 for i in range(2):
                     for way in range(2):
-                        for n in range(3):
-                            self.first(step, i, way, n).wait_send()
-                            self.last(step, i, way, n).wait_send()
+                        self.first_all(step, i, way).wait_send()
+                        self.last_all(step, i, way).wait_send()
 
     c_sum = Sum(
         c_cols,
@@ -426,12 +450,20 @@
     def g_first(step, i, way, n):
         on = on_x if way == 0 else on_z
         block = rows_in[i].at[step, way, z, x]
-        return copy_to(block, block, ss_g.at[step, i, way, n], rs_g.at[step, i, way, n], on[LINE[n]])
+        return copy_to(block, block, ss_g.at[step, i, way, 0], rs_g.at[step, i, way, 0], on[LINE[n]])
 
     def g_last(step, i, way, n):
         on = on_z if way == 0 else on_x
         block = rows_in[i].at[step, 0, z] if way == 0 else rows_in[i].at[step, 1, :, x]
-        return copy_to(block, block, ss_g.at[step, i, way, 3 + n], rs_g.at[step, i, way, 3 + n], on[LINE[n]])
+        return copy_to(block, block, ss_g.at[step, i, way, 1], rs_g.at[step, i, way, 1], on[LINE[n]])
+
+    def g_first_all(step, i, way):
+        return all_of(rows_in[i].at[step, way, 0, pl.ds(0, 3)],
+                      ss_g.at[step, i, way, 0], rs_g.at[step, i, way, 0], next_device)
+
+    def g_last_all(step, i, way):
+        return all_of(rows_in[i].at[step, way, pl.ds(0, 3)],
+                      ss_g.at[step, i, way, 1], rs_g.at[step, i, way, 1], next_device)
 
     def hidden(step, i):
         for way in range(2):
@@ -447,8 +479,7 @@
 
     def gather(step, i):
         for way in range(2):
-            for n in range(3):
-                g_first(step, i, way, n).wait_recv()
+            g_first_all(step, i, way).wait_recv()
             for n in range(3):
                 g_last(step, i, way, n).start()
 
@@ -456,8 +487,7 @@
         total = None
         squares = None
         for way in range(2):
-            for n in range(3):
-                g_last(step, i, way, n).wait_recv()
+            g_last_all(step, i, way).wait_recv()
             for m, col in enumerate(c_cols[i][way]):
                 rows = rows_in[i][step, way, :, :, :, m * 256:(m + 1) * 256].reshape(16, 16, 256)
                 a = unfold(rows.astype(F32)).reshape(128, 512)
@@ -545,12 +575,11 @@
     finish(1, 0)
     finish(1, 1)
 
-    for c in x_copies + p_copies + k_copies + m_copies:
+    for c in (x_all, p_all, k_all, m_all):
         c.wait_send()
 
     def drain(i, carry):
-        for c in a_copies(i // 2, i % 2):
-            c.wait_send()
+        a_all(i // 2, i % 2).wait_send()
         return carry
 
     lax.fori_loop(0, 4, drain, 0)
@@ -561,9 +590,8 @@
     for step in range(2):
         for i in range(2):
             for way in range(2):
-                for n in range(3):
-                    g_first(step, i, way, n).wait_send()
-                    g_last(step, i, way, n).wait_send()
+                g_first_all(step, i, way).wait_send()
+                g_last_all(step, i, way).wait_send()
 
 
 def layer(lengths, inputs, frequency, queries, cache, down_latent, value_up, output_weight, up_weight, down_weight):
@@ -613,8 +641,8 @@
                 pltpu.VMEM((2, 2, 3, 16, width), BF),
             ] + [pltpu.VMEM((2, 2, 4, 4, 16, width), BF)] * gathers
     scratch += [dma((8,)), dma((8,)), dma((7,)), dma((8,))]
-    scratch += [dma((15,))] * 4 + [dma((2, 2, 15))] * 2 + [dma((15,))] * 4 + [dma((10,))] * 2 + [dma((2, 2, 2, 6))] * 2
-    scratch += [dma((2, 2, 2, 3))] * 8
+    scratch += [dma] * 4 + [dma((2, 2))] * 2 + [dma] * 4 + [dma((10,))] * 2 + [dma((2, 2, 2, 2))] * 2
+    scratch += [dma((2, 2, 2))] * 8
     return pl.pallas_call(
         kernel,
         out_shape=jax.ShapeDtypeStruct((2, 8, D), BF),

time: 96.5 us -> 92.3 us (0.956)
  Pallas kernels: 94.3 us -> 90 us
    pallas_call x1, Pallas kernels: 94.3 us -> 90 us  [layer(): pl.pallas_call(kernel, out_shape=jax.ShapeDtypeStruct((2, 8, D), BF), in_...]
where the time goes in v3:
time: 92.3 us; the launch traced here: 91.6 us
  Pallas kernels  90 us (98%)
  local copies, waits for them, and re-layouts  1.57 us (2%)
    pallas_call x1, Pallas kernels, layer(): pl.pallas_call(kernel, out_shape=jax.ShapeDtypeStruct((2, 8, D), BF), in_...  90 us

profile of v3, /device:TPU:0, one launch (start us, length us, event | category | flops | bytes accessed | tf_op | source)
XLA Modules:
  0.0 91.6 jit_solution(17661148072067307495)
XLA Ops:
  0.0 90.0 %shard_map.100 = bf16[2,8,4096]{2,1,0:T(8,128)(2,1)} custom-call(s32[8]{0:T(128)} %lens.1, bf16[2,8,4096]{2,1,0:T(8,128)(2,1)} %x_hbm.1, f32[16,64]{1,0:T(8,128)} %constant.2.clone.freq_hbm, bf16[2,8,576,128]{3,2,1,0:T(8,128)(2,1)} %bitcast.6, bf16[8,576,512]{2,1,0:T(8,128)(2,1)} %bitcast.5, bf16[576,256]{1,0:T(8,128)(2,1)} %bitcast.7, ...), custom_call_target="tpu_custom_call" | custom-call | tf_op jit(solution)/shard_map/pallas_call | solution.py:646
  90.0 1.6 %copy.12 = bf16[2,8,4096]{2,1,0:T(8,128)(2,1)} copy(bf16[2,8,4096]{2,1,0:T(8,128)(2,1)} %shard_map.100) | data formatting | bytes 262144

commit v4 on v3

--- a/solution.py
+++ b/solution.py
@@ -138,8 +138,14 @@
     from_dn, from_up, from_far = y_dn * 2 + core, y_up * 2 + core, y_far * 2 + core
     w_up2 = copy_to(w_v.at[from_dn, lo], w_v.at[from_dn, lo], ss_w.at[5], rs_w.at[5], up_dev)
     w_dn2 = copy_to(w_v.at[from_up, hi], w_v.at[from_up, hi], ss_w.at[6], rs_w.at[6], dn_dev)
-    w_sib_dn = copy_to(w_v.at[from_dn], w_v.at[from_dn], ss_w.at[7], rs_w.at[7], sib_dev)
-    w_sib_up = copy_to(w_v.at[from_up], w_v.at[from_up], ss_w.at[8], rs_w.at[8], sib_dev)
+    w_sib_dn = [
+        copy_to(w_v.at[from_dn, s], w_v.at[from_dn, s], ss_w.at[7 + i], rs_w.at[7 + i], sib_dev)
+        for i, s in enumerate((lo, hi))
+    ]
+    w_sib_up = [
+        copy_to(w_v.at[from_up, s], w_v.at[from_up, s], ss_w.at[10 + i], rs_w.at[10 + i], sib_dev)
+        for i, s in enumerate((hi, lo))
+    ]
     w_sib_far = copy_to(w_v.at[from_far], w_v.at[from_far], ss_w.at[9], rs_w.at[9], sib_dev)
     for c in (w_up[0], w_dn[0], w_up[1], w_dn[1], w_sib):
         c.start()
@@ -192,6 +198,8 @@
         return carry
 
     lax.fori_loop(0, 1, attend_pair, 0)
+    for c in a_pair(0):
+        c.start()
 
     for c in vu_copies:
         c.start()
@@ -213,8 +221,6 @@
     for c in p_copies:
         c.start()
     p_all = all_of(pr, ss_p, rs_p, next_device)
-    for c in a_pair(0):
-        c.start()
 
     def attend_and_send(pair, carry):
         attend_pair(pair, carry)
@@ -516,13 +522,13 @@
 
     def weights_near():
         w_up[1].wait_recv()
+        w_sib_dn[1].start()
         w_dn[1].wait_recv()
-        w_sib_up.start()
-        w_sib_dn.start()
+        w_sib_up[1].start()
         ow_copy.wait()
         w_sib.wait_recv()
-        w_sib_up.wait_recv()
-        w_sib_dn.wait_recv()
+        for c in w_sib_up + w_sib_dn:
+            c.wait_recv()
 
     def weights_far():
         w_up2.wait_recv()
@@ -532,8 +538,10 @@
 
     w_up[0].wait_recv()
     w_up2.start()
+    w_sib_dn[0].start()
     w_dn[0].wait_recv()
     w_dn2.start()
+    w_sib_up[0].start()
     for c in vu_copies:
         c.wait()
     values(0)
@@ -583,7 +591,7 @@
         return carry
 
     lax.fori_loop(0, 4, drain, 0)
-    for c in w_up + w_dn + [w_sib, w_up2, w_dn2, w_sib_dn, w_sib_up, w_sib_far]:
+    for c in w_up + w_dn + w_sib_dn + w_sib_up + [w_sib, w_up2, w_dn2, w_sib_far]:
         c.wait_send()
     c_sum.drain()
     e_sum.drain()
@@ -641,7 +649,7 @@
                 pltpu.VMEM((2, 2, 3, 16, width), BF),
             ] + [pltpu.VMEM((2, 2, 4, 4, 16, width), BF)] * gathers
     scratch += [dma((8,)), dma((8,)), dma((7,)), dma((8,))]
-    scratch += [dma] * 4 + [dma((2, 2))] * 2 + [dma] * 4 + [dma((10,))] * 2 + [dma((2, 2, 2, 2))] * 2
+    scratch += [dma] * 4 + [dma((2, 2))] * 2 + [dma] * 4 + [dma((12,))] * 2 + [dma((2, 2, 2, 2))] * 2
     scratch += [dma((2, 2, 2))] * 8
     return pl.pallas_call(
         kernel,

time: 92.3 us -> 89.6 us (0.971)
  Pallas kernels: 90 us -> 87.9 us
    pallas_call x1, Pallas kernels: 90 us -> 87.9 us  [layer(): pl.pallas_call(kernel, out_shape=jax.ShapeDtypeStruct((2, 8, D), BF), in_...]
where the time goes in v4:
time: 89.6 us; the launch traced here: 89.5 us
  Pallas kernels  87.9 us (98%)
  local copies, waits for them, and re-layouts  1.57 us (2%)
    pallas_call x1, Pallas kernels, layer(): pl.pallas_call(kernel, out_shape=jax.ShapeDtypeStruct((2, 8, D), BF), in_...  87.9 us

profile of v4, /device:TPU:0, one launch (start us, length us, event | category | flops | bytes accessed | tf_op | source)
XLA Modules:
  0.0 89.5 jit_solution(6908945970498344187)
XLA Ops:
  0.0 87.9 %shard_map.100 = bf16[2,8,4096]{2,1,0:T(8,128)(2,1)} custom-call(s32[8]{0:T(128)} %lens.1, bf16[2,8,4096]{2,1,0:T(8,128)(2,1)} %x_hbm.1, f32[16,64]{1,0:T(8,128)} %constant.2.clone.freq_hbm, bf16[2,8,576,128]{3,2,1,0:T(8,128)(2,1)} %bitcast.6, bf16[8,576,512]{2,1,0:T(8,128)(2,1)} %bitcast.5, bf16[576,256]{1,0:T(8,128)(2,1)} %bitcast.7, ...), custom_call_target="tpu_custom_call" | custom-call | tf_op jit(solution)/shard_map/pallas_call | solution.py:654
  87.9 1.6 %copy.12 = bf16[2,8,4096]{2,1,0:T(8,128)(2,1)} copy(bf16[2,8,4096]{2,1,0:T(8,128)(2,1)} %shard_map.100) | data formatting | bytes 262144

commit v5 on v4

--- a/solution.py
+++ b/solution.py
@@ -108,7 +108,7 @@
     pl.semaphore_wait(barrier, len(partners))
 
     def x_slice(t):
-        return x_hbm.at[:, :, pl.ds(pl.multiple_of(t * 256, 256), 256)]
+        return x_hbm.at[:, pl.ds(pl.multiple_of(t * 256, 256), 256)]
 
     x_copies = [
         copy_to(x_slice(t), xr.at[tp], ss_x, rs_x, (dp, t))
@@ -210,7 +210,7 @@
     x_own.wait()
     x_all.wait_recv()
     partial = lax.dot_general(
-        xr[...].astype(F32).reshape(256, 256).astype(BF), dl_v[...], (((1,), (1,)), ((), ())),
+        xr[...].reshape(256, 256), dl_v[...], (((1,), (1,)), ((), ())),
         preferred_element_type=F32,
     )
     ps[...] = partial.astype(BF).reshape(16, 16, WIDTH)
@@ -232,7 +232,7 @@
 
     freq_copy.wait()
     x_copy.wait()
-    x0 = jnp.concatenate([x_in[0].astype(F32), x_in[1].astype(F32)], axis=0)
+    x0 = x_in[...].astype(F32)
     x_scale = lax.rsqrt(jnp.mean(x0 * x0, axis=-1, keepdims=True) + EPSILON)
     p_all.wait_recv()
     comp = ps[tp].astype(F32)
@@ -475,7 +475,7 @@
         for way in range(2):
             total = c_sum.end(step, i, way)
             for m, col in enumerate(c_cols[i][way]):
-                own = x_in[step, :, pl.ds(pl.multiple_of(col * 512, 512), 512)].astype(F32)
+                own = x_in[:, pl.ds(pl.multiple_of(col * 512, 512), 512)].astype(F32)[step * 8:step * 8 + 8]
                 here = slice(m * 256, (m + 1) * 256)
                 block = total[:, here] + fold(own)
                 hid[step, col] = block
@@ -606,7 +606,7 @@
     vmem, hbm = pl.BlockSpec(memory_space=pltpu.VMEM), pl.BlockSpec(memory_space=pl.ANY)
     dma = pltpu.SemaphoreType.DMA
     scratch = [
-        pltpu.VMEM((2, 8, D), BF),
+        pltpu.VMEM((16, D), BF),
         pltpu.VMEM((16, 64), F32),
         pltpu.VMEM((2, 8, WIDTH, 128), BF),
         pltpu.VMEM((8, WIDTH, CTX), BF),
@@ -615,7 +615,7 @@
         pltpu.VMEM((8, 1024, 512), BF),
         pltpu.VMEM((8, 512, FF), BF),
         pltpu.VMEM((FF, D), BF),
-        pltpu.VMEM((16, 2, 8, 256), BF),
+        pltpu.VMEM((16, 16, 256), BF),
         pltpu.VMEM((16, 16, WIDTH), BF),
         pltpu.VMEM((15, 16, WIDTH), BF),
         pltpu.VMEM((16, WIDTH), BF),
@@ -667,7 +667,7 @@
     half = ROPE_BASE ** (-np.arange(32, dtype=np.float32) / np.float32(32))
     frequency = np.tile(half.astype(np.float32), (16, 2))
     return layer(
-        lengths, inputs, jnp.asarray(frequency),
+        lengths, inputs.reshape(16, D), jnp.asarray(frequency),
         jnp.swapaxes(queries, 2, 3), jnp.swapaxes(latent_cache, 1, 2), down_latent.T,
         value_up, output_weight, up_weight.reshape(8, 512, FF), down_weight,
     )

time: 89.6 us -> 89.6 us (level)
  no operation moved by 1% of the time
where the time goes in v5:
time: 89.6 us; the launch traced here: 89.5 us
  Pallas kernels  87.9 us (98%)
  local copies, waits for them, and re-layouts  1.57 us (2%)
    pallas_call x1, Pallas kernels, layer(): pl.pallas_call(kernel, out_shape=jax.ShapeDtypeStruct((2, 8, D), BF), in_...  87.9 us

profile of v5, /device:TPU:0, one launch (start us, length us, event | category | flops | bytes accessed | tf_op | source)
XLA Modules:
  0.0 89.5 jit_solution(6908945970498344187)
XLA Ops:
  0.0 87.9 %shard_map.100 = bf16[2,8,4096]{2,1,0:T(8,128)(2,1)} custom-call(s32[8]{0:T(128)} %lens.1, bf16[16,4096]{1,0:T(8,128)(2,1)} %bitcast.9, f32[16,64]{1,0:T(8,128)} %constant.2.clone.freq_hbm, bf16[2,8,576,128]{3,2,1,0:T(8,128)(2,1)} %bitcast.7, bf16[8,576,512]{2,1,0:T(8,128)(2,1)} %bitcast.6, bf16[576,256]{1,0:T(8,128)(2,1)} %bitcast.8, ...), custom_call_target="tpu_custom_call" | custom-call | tf_op jit(solution)/shard_map/pallas_call | solution.py:654
  87.9 1.6 %copy.12 = bf16[2,8,4096]{2,1,0:T(8,128)(2,1)} copy(bf16[2,8,4096]{2,1,0:T(8,128)(2,1)} %shard_map.100) | data formatting | bytes 262144

commit v6 on v5

--- a/solution.py
+++ b/solution.py
@@ -281,7 +281,7 @@
         mix = jnp.where(lane == r, cached * inverse, mix)
         return jnp.where(lane == r + 8, p0 * inverse, mix)
 
-    mix = lax.fori_loop(0, 8, mix_row, jnp.zeros((128, 128), F32))
+    mix = lax.fori_loop(0, 8, mix_row, jnp.zeros((128, 128), F32), unroll=True)
     mix_s[...] = mix.reshape(16, 8, 128)
     mix_r[tp] = mix_s[tp]
     m_copies = [

time: 89.6 us -> 89.6 us (level)
  no operation moved by 1% of the time
where the time goes in v6:
time: 89.6 us; the launch traced here: 89.5 us
  Pallas kernels  87.9 us (98%)
  local copies, waits for them, and re-layouts  1.57 us (2%)
    pallas_call x1, Pallas kernels, layer(): pl.pallas_call(kernel, out_shape=jax.ShapeDtypeStruct((2, 8, D), BF), in_...  87.9 us

profile of v6, /device:TPU:0, one launch (start us, length us, event | category | flops | bytes accessed | tf_op | source)
XLA Modules:
  0.0 89.5 jit_solution(4997658301550672564)
XLA Ops:
  0.0 87.9 %shard_map.100 = bf16[2,8,4096]{2,1,0:T(8,128)(2,1)} custom-call(s32[8]{0:T(128)} %lens.1, bf16[16,4096]{1,0:T(8,128)(2,1)} %bitcast.9, f32[16,64]{1,0:T(8,128)} %constant.2.clone.freq_hbm, bf16[2,8,576,128]{3,2,1,0:T(8,128)(2,1)} %bitcast.7, bf16[8,576,512]{2,1,0:T(8,128)(2,1)} %bitcast.6, bf16[576,256]{1,0:T(8,128)(2,1)} %bitcast.8, ...), custom_call_target="tpu_custom_call" | custom-call | tf_op jit(solution)/shard_map/pallas_call | solution.py:654
  87.9 1.6 %copy.12 = bf16[2,8,4096]{2,1,0:T(8,128)(2,1)} copy(bf16[2,8,4096]{2,1,0:T(8,128)(2,1)} %shard_map.100) | data formatting | bytes 262144
